TPU v7x, 128 devices: a whole 4x4x4 slice. The times are simulated.
128 devices in a mesh: inner: 16 (over x, z_lo, core), outer: 8 (over z_hi, y).
Axes of the slice: x: 4, y: 4, z: 4 (z_hi: 2, z_lo: 2; z = z_hi * 2 + z_lo), core: 2. Of those that a mesh axis runs over, the one named last changes fastest.
Arguments:
- queries: bfloat16 [16384, 1024], P(('inner', 'outer')), may hold values from -8 to 8
- keys: bfloat16 [16384, 128], P(('inner', 'outer')), may hold values from -8 to 8
- values: bfloat16 [16384, 128], P(('inner', 'outer')), may hold values from -6 to 6
- outputs: bfloat16 [16384, 1024], P(('inner', 'outer')), may hold values from -6 to 6
- out_grad: bfloat16 [16384, 1024], P(('inner', 'outer')), may hold values from -6 to 6
- block_order: int32 [256], replicated, may hold values from 0 to 255, each once
Outputs:
- query_grad: bfloat16 [16384, 1024], P(('inner', 'outer'))
- key_grad: float32 [16384, 128], P(('inner', 'outer'))
- value_grad: float32 [16384, 128], P(('inner', 'outer'))
Inputs may be any that keep to these rules, and one draw needn't show every extreme that they name: `block_order`: each block number appears once.
All inputs are finite; a program needn't handle non-finite values.
Results may differ from a plain program's by a relative error of at most 0.015.
Values may be sent and summed in bfloat16 or wider, within the bound.
No kernel may reach another device: no remote copies, remote signals or barrier semaphores. Data moves between devices by JAX's collectives and lax.ppermute only.
A program may use at most 128 MiB of HBM per device.

v0:
```python
import math

import jax
import jax.numpy as jnp
from jax import lax
from jax.sharding import PartitionSpec as P


def block_length(count, query_count, heads):
    target = max(8, 1048576 // (query_count * heads))
    return math.gcd(count, target)


def softmax_totals(carry, query_rows, key_piece, key_pos, own_pos, scale):
    count = key_piece.shape[0]
    sub = block_length(count, query_rows.shape[0], query_rows.shape[1])
    pieces = key_piece.reshape(count // sub, sub, key_piece.shape[1])
    places = key_pos.reshape(count // sub, sub)

    def inner_step(state, item):
        top, total = state
        block_keys, block_pos = item
        scores = (
            jnp.einsum("qhd,kd->qhk", query_rows, block_keys, preferred_element_type=jnp.float32)
            * scale
        )
        scores = jnp.where(block_pos[None, None, :] <= own_pos[:, None, None], scores, -jnp.inf)
        new_top = jnp.maximum(top, jnp.max(scores, axis=2))
        total = total * jnp.exp(top - new_top) + jnp.sum(
            jnp.exp(scores - new_top[:, :, None]), axis=2
        )
        return ((new_top, total), None)

    result, unused = lax.scan(inner_step, carry, (pieces, places))
    return result


def tile_grads(query_rows, grad_rows, delta, lse, own_pos, key_all, value_all, key_pos, scale):
    total_rows, width = key_all.shape
    kblock = block_length(total_rows, query_rows.shape[0], query_rows.shape[1])
    key_blocks = key_all.reshape(total_rows // kblock, kblock, width)
    value_blocks = value_all.reshape(total_rows // kblock, kblock, width)
    pos_blocks = key_pos.reshape(total_rows // kblock, kblock)

    def main_step(query_acc, item):
        block_keys, block_values, block_pos = item
        scores = (
            jnp.einsum("qhd,kd->qhk", query_rows, block_keys, preferred_element_type=jnp.float32)
            * scale
        )
        visible = block_pos[None, None, :] <= own_pos[:, None, None]
        prob = jnp.where(visible, jnp.exp(scores - lse[:, :, None]), 0.0)
        probs = prob.astype(jnp.bfloat16)
        dprob = jnp.einsum(
            "qhd,kd->qhk", grad_rows, block_values, preferred_element_type=jnp.float32
        )
        grads = (prob * (dprob - delta[:, :, None]) * scale).astype(jnp.bfloat16)
        query_acc = query_acc + jnp.einsum(
            "qhk,kd->qhd", grads, block_keys, preferred_element_type=jnp.float32
        )
        key_term = jnp.einsum("qhk,qhd->kd", grads, query_rows, preferred_element_type=jnp.float32)
        value_term = jnp.einsum("qhk,qhd->kd", probs, grad_rows, preferred_element_type=jnp.float32)
        return (query_acc, (key_term, value_term))

    start_acc = jnp.zeros(query_rows.shape, jnp.float32)
    query_acc, (key_terms, value_terms) = lax.scan(
        main_step, start_acc, (key_blocks, value_blocks, pos_blocks)
    )
    return (query_acc, key_terms.reshape(total_rows, width), value_terms.reshape(total_rows, width))


def shards(queries, keys, values, outputs, out_grad, block_order):
    rows = queries.shape[0]
    width = keys.shape[1]
    heads = queries.shape[1] // width
    scale = width ** (-0.5)
    nblocks = block_order.shape[0]
    block = rows // 2
    position = jnp.repeat(block_order, block) * block + jnp.tile(
        jnp.arange(block, dtype=jnp.int32), nblocks
    )
    grad_rows = out_grad.reshape(rows, heads, width)
    out_rows = outputs.reshape(rows, heads, width)
    delta = jnp.sum(grad_rows.astype(jnp.float32) * out_rows.astype(jnp.float32), axis=2)
    device = lax.axis_index(("inner", "outer"))
    own_pos = lax.dynamic_slice_in_dim(position, device * rows, rows, 0)
    query_rows = queries.reshape(rows, heads, width)
    key_all, value_all = (
        lax.all_gather(keys, ("inner", "outer"), axis=0, tiled=True),
        lax.all_gather(values, ("inner", "outer"), axis=0, tiled=True),
    )
    start_state = (
        jnp.full((rows, heads), -1e30, jnp.float32),
        jnp.zeros((rows, heads), jnp.float32),
    )
    top, total = softmax_totals(start_state, query_rows, key_all, position, own_pos, scale)
    lse = top + jnp.log(total)
    query_acc, key_terms, value_terms = tile_grads(
        query_rows, grad_rows, delta, lse, own_pos, key_all, value_all, position, scale
    )
    query_grad = query_acc.astype(jnp.bfloat16).reshape(rows, heads * width)
    key_grad, value_grad = (
        lax.psum_scatter(key_terms, ("inner", "outer"), scatter_dimension=0, tiled=True),
        lax.psum_scatter(value_terms, ("inner", "outer"), scatter_dimension=0, tiled=True),
    )
    return (query_grad, key_grad, value_grad)


def solution(mesh):
    placed = (
        P(("inner", "outer"), None),
        P(("inner", "outer"), None),
        P(("inner", "outer"), None),
        P(("inner", "outer"), None),
        P(("inner", "outer"), None),
        P(),
    )
    return jax.shard_map(
        shards,
        mesh=mesh,
        in_specs=placed,
        out_specs=(
            P(("inner", "outer"), None),
            P(("inner", "outer"), None),
            P(("inner", "outer"), None),
        ),
        check_vma=False,
    )
```

profile of v0, /device:TPU:1, one launch (start us, length us, event | category | flops | bytes accessed | tf_op | source)
XLA Modules:
  0.0 2073.4 jit_solution(13909952685900399404)
XLA Ops:
  13.9 305.9 %all-gather.3.cloned.1.call-done = bf16[16384,128]{1,0:T(8,128)(2,1)} async-done(((bf16[128,128]{1,0:T(8,128)(2,1)}), bf16[16384,128]{1,0:T(8,128)(2,1)}) %all-gather.3.cloned.1.call-update) | async-done | bytes 4194320 | tf_op jit(solution)/shard_map/all_gather | solution.py:89
  319.8 45.3 %while.28 = (s32[]{:T(128)}, f32[128,8]{0,1:T(8,128)S(1)}, f32[128,8]{0,1:T(8,128)S(1)}, s32[16,1024]{1,0:T(8,128)S(1)}, s32[128]{0:T(128)S(1)}, /*index=5*/bf16...) while((s32[]{:T(128)}, f32[128,8]{0,1:T(8,128)S(1)}, ...), condition=%wide.region_3.4_spmd.clone, body=%wide.region_0.3_spmd.clone.sunk | while | flops 275911680 | bytes 9372280 | solution.py:34
  320.0 1.7 fusion.57
  322.8 1.7 fusion.57
  325.7 1.7 fusion.57
  328.5 1.7 fusion.57
  331.3 1.7 fusion.57
  334.2 1.7 fusion.57
  337.0 1.7 fusion.57
  339.9 1.7 fusion.57
  342.7 1.7 fusion.57
  345.5 1.7 fusion.57
  348.4 1.7 fusion.57
  351.2 1.7 fusion.57
  354.0 1.7 fusion.57
  356.9 1.7 fusion.57
  359.7 1.7 fusion.57
  362.5 1.7 fusion.57
  365.1 264.1 %all-gather.5.cloned.1.call-done = bf16[16384,128]{1,0:T(8,128)(2,1)} async-done(((bf16[128,128]{1,0:T(8,128)(2,1)}), bf16[16384,128]{1,0:T(8,128)(2,1)}) %all-gather.5.cloned.1.call-update) | async-done | bytes 4194320 | tf_op jit(solution)/shard_map/all_gather | solution.py:90
  629.2 150.0 %while.29 = (s32[]{:T(128)}, f32[128,8,128]{2,0,1:T(8,128)S(1)}, f32[16,1024,128]{2,1,0:T(8,128)}, f32[16,1024,128]{2,1,0:T(8,128)}, s32[16,1024]{1,0:T(8,128)S(...) while((s32[]{:T(128)}, f32[128,8,128]{2,0,1:T(8,128)S(1)}, ...), condition=%wide.region_6.7_spmd.clone, body=%wide.region_5.6_spmd.clone.sunk | while | flops 1354104832 | bytes 23225008 | solution.py:66
  631.1 2.5 fusion.70
  633.5 1.8 convolution_add_fusion.2
  635.4 1.7 fusion.72
  638.8 1.7 fusion.69
  640.5 2.4 fusion.70
  642.9 1.8 convolution_add_fusion.2
  644.8 1.7 fusion.72
  648.2 1.7 fusion.69
  649.9 2.4 fusion.70
  652.4 1.8 convolution_add_fusion.2
  659.3 2.5 fusion.70
  661.7 1.8 convolution_add_fusion.2
  668.6 2.5 fusion.70
  671.1 1.8 convolution_add_fusion.2
  672.9 1.7 fusion.72
  676.3 1.7 fusion.69
  678.0 2.5 fusion.70
  680.5 1.8 convolution_add_fusion.2
  687.4 2.5 fusion.70
  689.8 1.8 convolution_add_fusion.2
  696.7 2.5 fusion.70
  699.2 1.8 convolution_add_fusion.2
  706.1 2.5 fusion.70
  708.6 1.8 convolution_add_fusion.2
  710.4 1.7 fusion.72
  715.5 2.5 fusion.70
  717.9 1.8 convolution_add_fusion.2
  719.8 1.7 fusion.72
  724.9 2.5 fusion.70
  727.3 1.8 convolution_add_fusion.2
  734.2 2.5 fusion.70
  736.7 1.8 convolution_add_fusion.2
  743.6 2.5 fusion.70
  746.0 1.8 convolution_add_fusion.2
  747.9 1.7 fusion.72
  753.0 2.5 fusion.70
  755.4 1.8 convolution_add_fusion.2
  757.3 1.7 fusion.72
  762.4 2.5 fusion.70
  764.8 1.8 convolution_add_fusion.2
  771.7 2.5 fusion.70
  774.2 1.8 convolution_add_fusion.2
  780.5 637.1 %reduce-scatter.5.cloned.1.call-done = f32[128,128]{1,0:T(8,128)} async-done(((f32[16384,128]{1,0:T(8,128)}), f32[128,128]{1,0:T(8,128)}) %reduce-scatter.5.cloned.1.call-update) | async-done | bytes 65552 | tf_op jit(solution)/shard_map/reduce_scatter | solution.py:104
  1417.7 649.2 %reduce-scatter.3.cloned.1.call-done = f32[128,128]{1,0:T(8,128)} async-done(((f32[16384,128]{1,0:T(8,128)}), f32[128,128]{1,0:T(8,128)}) %reduce-scatter.3.cloned.1.call-update) | async-done | bytes 65552 | tf_op jit(solution)/shard_map/reduce_scatter | solution.py:103
  (197 shorter events, 89.4 us)
Async XLA Ops:
  7.2 312.6 %all-gather.3.cloned.1.call-start = ((), (), s32[]{:S(2)}) async-start(), calls=%async_computation.2 | async-start | bytes 4227072 | tf_op jit(solution)/shard_map/all_gather | solution.py:89
  7.9 621.3 %all-gather.5.cloned.1.call-start = ((), (), s32[]{:S(2)}) async-start(), calls=%async_computation.3 | async-start | bytes 4227072 | tf_op jit(solution)/shard_map/all_gather | solution.py:90
  8.6 1409.0 %reduce-scatter.5.cloned.1.call-start = ((), (), s32[]{:S(2)}) async-start(), calls=%async_computation.5 | async-start | bytes 8454144 | tf_op jit(solution)/shard_map/reduce_scatter | solution.py:104
  779.2 1287.6 %reduce-scatter.3.cloned.1.call-start = ((), (), s32[]{:S(2)}) async-start(), calls=%async_computation.4 | async-start | bytes 8454144 | tf_op jit(solution)/shard_map/reduce_scatter | solution.py:103
Sparse Core Ops, SparseCore 0:
  9.7 310.0 all-gather.2
  321.5 307.6 all-gather.4
  779.3 638.2 reduce-scatter.4
  1420.6 646.2 reduce-scatter.2
where the time goes:
time: 2090 us; the launch traced here: 2070 us
  waiting for transfers between devices  1860 us (89%)
  matrix products  173 us (8%)
  other arithmetic  22.2 us (1%)
    reduce_scatter x1, waiting for transfers between devices, shards(): lax.psum_scatter(key_terms, ('inner', 'outer'), scatter_dimension=0, tile...  649 us
    reduce_scatter x1, waiting for transfers between devices, shards(): lax.psum_scatter(value_terms, ('inner', 'outer'), scatter_dimension=0, ti...  637 us
    all_gather x1, waiting for transfers between devices, shards(): lax.all_gather(keys, ('inner', 'outer'), axis=0, tiled=True)  306 us
    all_gather x1, waiting for transfers between devices, shards(): lax.all_gather(values, ('inner', 'outer'), axis=0, tiled=True)  264 us
  transfers between devices with their start and end apart: 4, of which 4 were waited for; matrix products, arithmetic and copies ran while one was open for 2% of the time, Pallas kernels for 0%

commit v1 on v0

v1 whole, which is shorter than its diff:
```python
import functools
import math

import jax
import jax.numpy as jnp
from jax import lax
from jax.experimental import pallas as pl
from jax.experimental.pallas import tpu as pltpu
from jax.sharding import Mesh, PartitionSpec as P

DH = 128
HEADS = 8
BLOCK = 64
ROWS = HEADS * BLOCK
SCALE = DH ** -0.5
C2 = SCALE * math.log2(math.e)
NEG = -1e30
KB = 8
KT = KB * BLOCK
VMEM_LIMIT = 56 * 1024 * 1024
F32 = jnp.float32
BF16 = jnp.bfloat16
KEY_AXES = ("x", "zl", "zh")


def nn(a, b):
    return lax.dot_general(a, b, (((1,), (0,)), ((), ())), preferred_element_type=F32)


def sort_blocks(rank_ref, src, dst, nk):
    def body(j, c):
        r = pl.multiple_of(rank_ref[j] * BLOCK, BLOCK)
        dst[pl.ds(r, BLOCK), :] = src[pl.ds(pl.multiple_of(j * BLOCK, BLOCK), BLOCK), :]
        return c

    lax.fori_loop(0, nk, body, 0)


def causal(s, place_ref, t, query_place, diff):
    parts = []
    for u in range(KB):
        place = place_ref[t * KB + u]
        limit = jnp.where(place < query_place, BLOCK, jnp.where(place == query_place, 0, -2 * BLOCK))
        parts.append(jnp.where(diff <= limit, s[u * BLOCK:(u + 1) * BLOCK], 2 * NEG))
    return jnp.concatenate(parts, 0)


def difference():
    key = lax.broadcasted_iota(jnp.int32, (BLOCK, ROWS), 0)
    query = lax.broadcasted_iota(jnp.int32, (BLOCK, ROWS), 1) % BLOCK
    return key - query


def for_tiles(n, tile):
    whole = jnp.maximum(n - 1, 0) // KB

    def step(t, c):
        tile(t, False)
        return c

    lax.fori_loop(0, whole, step, 0)

    @pl.when(n > 0)
    def _():
        tile(whole, True)


def lse_kernel(nq, nk, rank_ref, place_ref, n_ref, qp_ref, qg_ref, k_ref, lse_ref, ks, m8, l8):
    sort_blocks(rank_ref, k_ref, ks, nk)

    def block(b, c):
        m8[...] = jnp.full_like(m8, NEG)
        l8[...] = jnp.zeros_like(l8)

        def tile(t, last):
            keys = ks[pl.ds(pl.multiple_of(t * KT, KT), KT), :]
            s = nn(keys, qg_ref[b, :DH, :]) * C2
            if last:
                s = causal(s, place_ref, t, qp_ref[b], difference())
            s = s.reshape(KT // 8, 8, ROWS)
            m = m8[...]
            top = jnp.maximum(m, jnp.max(s, axis=0))
            l8[...] = l8[...] * jnp.exp2(m - top) + jnp.sum(jnp.exp2(s - top[None]), axis=0)
            m8[...] = top

        for_tiles(n_ref[b], tile)
        m = m8[...]
        top = jnp.max(m, axis=0, keepdims=True)
        total = jnp.sum(l8[...] * jnp.exp2(m - top), axis=0, keepdims=True)
        lse_ref[b] = jnp.where(total > 0, top + jnp.log2(jnp.maximum(total, 1e-37)), NEG)
        return c

    lax.fori_loop(0, nq, block, 0)


def local_lse(scalars, qg, keys):
    nq = qg.shape[0]
    count = keys.shape[0]
    smem = pl.BlockSpec(memory_space=pltpu.SMEM)
    vmem = pl.BlockSpec(memory_space=pltpu.VMEM)
    return pl.pallas_call(
        functools.partial(lse_kernel, nq, count // BLOCK),
        out_shape=jax.ShapeDtypeStruct((nq, 1, ROWS), F32),
        in_specs=[smem] * 4 + [vmem] * 2,
        out_specs=vmem,
        scratch_shapes=[
            pltpu.VMEM((count, DH), BF16),
            pltpu.VMEM((8, ROWS), F32),
            pltpu.VMEM((8, ROWS), F32),
        ],
        compiler_params=pltpu.CompilerParams(vmem_limit_bytes=VMEM_LIMIT),
        name="local_lse",
    )(*scalars, qg, keys)


def grad_kernel(
    nq, nk, rank_ref, place_ref, n_ref, qp_ref, qg_ref, lse_ref, k_ref, v_ref,
    dq_ref, dkv_ref, ks, vs, kst, dka, dva, dqa, qn, gn,
):
    sort_blocks(rank_ref, k_ref, ks, nk)
    sort_blocks(rank_ref, v_ref, vs, nk)
    kst[...] = ks[...].T
    dka[...] = jnp.zeros_like(dka)
    dva[...] = jnp.zeros_like(dva)

    def block(b, c):
        dqa[...] = jnp.zeros_like(dqa)
        qn[...] = qg_ref[b, :DH, :].T
        gn[...] = qg_ref[b, DH:2 * DH, :].T
        lse = lse_ref[b]
        delta = qg_ref[b, 2 * DH:, :].astype(F32)
        delta = delta[0:1] + delta[1:2] + delta[2:3]

        def tile(t, last):
            at = pl.ds(pl.multiple_of(t * KT, KT), KT)
            s = nn(ks[at, :], qg_ref[b, :DH, :]) * C2 - lse
            if last:
                s = causal(s, place_ref, t, qp_ref[b], difference())
            p = jnp.exp2(s)
            dp = nn(vs[at, :], qg_ref[b, DH:2 * DH, :])
            ds = (p * (dp - delta)).astype(BF16)
            dqa[...] += nn(kst[:, at], ds)
            dva[at, :] += nn(p.astype(BF16), gn[...])
            dka[at, :] += nn(ds, qn[...])

        for_tiles(n_ref[b], tile)
        dq_ref[b] = dqa[...] * SCALE
        return c

    lax.fori_loop(0, nq, block, 0)

    def body(j, c):
        r = pl.ds(pl.multiple_of(rank_ref[j] * BLOCK, BLOCK), BLOCK)
        at = pl.ds(pl.multiple_of(j * BLOCK, BLOCK), BLOCK)
        dkv_ref[at, :DH] = (dka[r, :] * SCALE).astype(dkv_ref.dtype)
        dkv_ref[at, DH:] = dva[r, :].astype(dkv_ref.dtype)
        return c

    lax.fori_loop(0, nk, body, 0)


def local_grads(scalars, qg, lse, keys, values):
    nq = qg.shape[0]
    count = keys.shape[0]
    smem = pl.BlockSpec(memory_space=pltpu.SMEM)
    vmem = pl.BlockSpec(memory_space=pltpu.VMEM)
    return pl.pallas_call(
        functools.partial(grad_kernel, nq, count // BLOCK),
        out_shape=(
            jax.ShapeDtypeStruct((nq, DH, ROWS), F32),
            jax.ShapeDtypeStruct((count, 2 * DH), BF16),
        ),
        in_specs=[smem] * 4 + [vmem] * 4,
        out_specs=(vmem, vmem),
        scratch_shapes=[
            pltpu.VMEM((count, DH), BF16),
            pltpu.VMEM((count, DH), BF16),
            pltpu.VMEM((DH, count), BF16),
            pltpu.VMEM((count, DH), F32),
            pltpu.VMEM((count, DH), F32),
            pltpu.VMEM((DH, ROWS), F32),
            pltpu.VMEM((ROWS, DH), BF16),
            pltpu.VMEM((ROWS, DH), BF16),
        ],
        compiler_params=pltpu.CompilerParams(vmem_limit_bytes=VMEM_LIMIT),
        name="local_grads",
    )(*scalars, qg, lse, keys, values)


def along(axis, shift, size, array):
    return lax.ppermute(array, axis, [(i, (i + shift) % size) for i in range(size)])


def combine(parts):
    top = functools.reduce(jnp.maximum, parts)
    return top + jnp.log2(sum(jnp.exp2(part - top) for part in parts))


def shards(queries, keys, values, outputs, out_grad, block_order):
    y = lax.axis_index("y")
    core = lax.axis_index("core")

    def columns(a):
        return a.reshape(2, BLOCK, HEADS, DH).transpose(0, 3, 2, 1).reshape(2, DH, ROWS)

    product = out_grad.astype(F32) * outputs.astype(F32)
    delta = jnp.sum(product.reshape(2, BLOCK, HEADS, DH), axis=3).transpose(0, 2, 1).reshape(2, 1, ROWS)
    d1 = lax.reduce_precision(delta, 8, 7)
    d2 = lax.reduce_precision(delta - d1, 8, 7)
    d3 = delta - d1 - d2
    extra = jnp.concatenate([d1, d2, d3, jnp.zeros((2, 13, ROWS), F32)], axis=1).astype(BF16)
    own = jnp.concatenate([columns(queries), columns(out_grad), extra], axis=1)

    pair = jnp.concatenate([keys, values], axis=1)
    gathered = lax.all_to_all(jnp.tile(pair, (16, 1)), KEY_AXES, 0, 0, tiled=True)
    key_all, value_all = gathered[:, :DH], gathered[:, DH:]

    pieces = [own] + [along("y", s, 4, own) for s in (1, 2, 3)]
    mine = jnp.stack(pieces)
    other = along("core", 1, 2, mine)
    qg = jnp.stack([mine, other], axis=1).reshape(16, 2 * DH + 16, ROWS)

    order = block_order.reshape(4, 2, 2, 2, 4, 2)
    key_place = lax.dynamic_slice(order, (0, 0, core, 0, y, 0), (4, 2, 1, 2, 1, 2)).reshape(32)
    here = lax.dynamic_slice(
        order, (lax.axis_index("x"), lax.axis_index("zl"), 0, lax.axis_index("zh"), 0, 0), (1, 1, 2, 1, 4, 2)
    ).reshape(2, 4, 2)
    query_place = jnp.stack(
        [jnp.stack([here[core ^ c, (y - s) % 4] for c in range(2)]) for s in range(4)]
    ).reshape(16)
    before = key_place[:, None] < key_place[None, :]
    rank = jnp.sum(before, axis=0, dtype=jnp.int32)
    spots = lax.broadcasted_iota(jnp.int32, (32, 32), 0)
    place = jnp.sum(jnp.where(rank[None, :] == spots, key_place[None, :], 0), axis=1, dtype=jnp.int32)
    visible = jnp.sum(key_place[None, :] <= query_place[:, None], axis=1, dtype=jnp.int32)
    scalars = (rank, place, visible, query_place)

    part = local_lse(scalars, qg, key_all).reshape(4, 2, 2, ROWS)
    part = combine([part, along("core", 1, 2, part)[:, ::-1]])
    around = [part]
    for d in (1, 2, 3):
        peer = along("y", -d, 4, part)
        around.append(jnp.roll(peer, -d, axis=0))
    lse = combine(around).reshape(16, 1, ROWS)

    query_part, kv_part = local_grads(scalars, qg, lse, key_all, value_all)

    query_part = query_part.reshape(4, 2, 2, DH, ROWS)
    query_sum = query_part[:, 0] + along("core", 1, 2, query_part[:, 1])
    total = query_sum[0]
    for s in (1, 2, 3):
        total = total + along("y", -s, 4, query_sum[s].astype(BF16)).astype(F32)
    query_grad = total.astype(BF16).reshape(2, DH, HEADS, BLOCK).transpose(0, 3, 2, 1).reshape(2 * BLOCK, HEADS * DH)

    terms = lax.all_to_all(kv_part, KEY_AXES, 0, 0, tiled=True)
    kv_grad = jnp.sum(terms.astype(F32).reshape(16, 2 * BLOCK, 2 * DH), axis=0)
    return query_grad, kv_grad[:, :DH], kv_grad[:, DH:]


def solution(mesh):
    fine = Mesh(mesh.devices.reshape(4, 2, 2, 2, 4), ("x", "zl", "core", "zh", "y"))
    rows = P(("x", "zl", "core", "zh", "y"), None)
    return jax.shard_map(
        shards,
        mesh=fine,
        in_specs=(rows,) * 5 + (P(),),
        out_specs=(rows,) * 3,
        check_vma=False,
    )
```

time: 2090 us -> 217 us (0.10)
  waiting for transfers between devices: 1860 us -> 50.1 us
  matrix products: 173 us -> 0 us
  Pallas kernels: 0 us -> 71.5 us
  starting transfers between devices: 0.16 us -> 35 us
  local copies, waits for them, and re-layouts: 4.56 us -> 38.8 us
    reduce_scatter x2 -> x0, waiting for transfers between devices: 1290 us -> none  [the longest x1 649 us: shards(): lax.psum_scatter(key_terms, ('inner', 'outer'), scatter_dimension=0, tile...]
    all_gather x2 -> x0, waiting for transfers between devices: 570 us -> none  [the longest x1 306 us: shards(): lax.all_gather(keys, ('inner', 'outer'), axis=0, tiled=True)]
    dot_general x96 -> x0, matrix products: 173 us -> none  [the longest x16 39.3 us: main_step(): jnp.einsum('qhd,kd->qhk', grad_rows, block_values, preferred_element_type...]
    pallas_call x0 -> x2, Pallas kernels: none -> 71.5 us  [the longest x1 46.8 us: local_grads(): pl.pallas_call(functools.partial(grad_kernel, nq, count // BLOCK), out_sh...]
    ppermute x0 -> x12, waiting for transfers between devices: none -> 29 us  [along(): lax.ppermute(array, axis, [(i, (i + shift) % size) for i in range(size)])]
    all_to_all x0 -> x2, waiting for transfers between devices: none -> 21.1 us  [the longest x1 16 us: shards(): lax.all_to_all(jnp.tile(pair, (16, 1)), KEY_AXES, 0, 0, tiled=True)]
  transfers between devices with their start and end apart: 4 -> 14, of which waited for: 4 -> 9; matrix products, arithmetic and copies ran while one was open for 2% -> 6% of each run, Pallas kernels for 0% -> 0%
where the time goes in v1:
time: 217 us; the launch traced here: 214 us
  Pallas kernels  71.5 us (33%)
  waiting for transfers between devices  50.1 us (23%)
  local copies, waits for them, and re-layouts  38.8 us (18%)
  starting transfers between devices  35 us (16%)
  other arithmetic  17.6 us (8%)
    pallas_call x1, Pallas kernels, local_grads(): pl.pallas_call(functools.partial(grad_kernel, nq, count // BLOCK), out_sh...  46.8 us
    ppermute x12, waiting for transfers between devices, along(): lax.ppermute(array, axis, [(i, (i + shift) % size) for i in range(size)])  29 us
    pallas_call x1, Pallas kernels, local_lse(): pl.pallas_call(functools.partial(lse_kernel, nq, count // BLOCK), out_sha...  24.6 us
    ppermute x12, starting transfers between devices, along(): lax.ppermute(array, axis, [(i, (i + shift) % size) for i in range(size)])  17.9 us
    all_to_all x1, waiting for transfers between devices, shards(): lax.all_to_all(jnp.tile(pair, (16, 1)), KEY_AXES, 0, 0, tiled=True)  16 us
    all_to_all x1, starting transfers between devices, shards(): terms = lax.all_to_all(kv_part, KEY_AXES, 0, 0, tiled=True)  9.47 us
    another operation x2, other arithmetic, shards(): qg = jnp.stack([mine, other], axis=1).reshape(16, 2 * DH + 16, ROWS)  9.17 us
    ppermute x4, local copies, waits for them, and re-layouts, along(): lax.ppermute(array, axis, [(i, (i + shift) % size) for i in range(size)])  8.08 us
  transfers between devices with their start and end apart: 14, of which 9 were waited for; matrix products, arithmetic and copies ran while one was open for 6% of the time, Pallas kernels for 0%

profile of v1, /device:TPU:1, one launch (start us, length us, event | category | flops | bytes accessed | tf_op | source)
XLA Modules:
  0.0 214.1 jit_solution(5851670424940510018)
XLA Ops:
  0.7 1.1 multiply_bitcast_fusion
  1.8 0.1 copy.82
  1.9 0.2 bitcast_reduce_fusion
  2.1 0.1 copy.61
  2.2 0.1 reshape.130
  2.3 0.2 copy.62
  2.5 0.2 copy.63
  2.7 0.2 copy.64
  3.2 2.9 %concatenate.21 = bf16[2,272,512]{1,2,0:T(8,128)(2,1)S(1)} concatenate(bf16[2,128,512]{1,2,0:T(8,128)(2,1)S(1)} %bitcast.96, bf16[2,128,512]{1,2,0:T(8,128)(2,1)S(1)} %bitcast.97, bf16[2,1,512]{1,2,0:T(8,128)(2,1)S(1)} %copy.62, bf16[2,1,512]{1,2,0:T(8,128)(2,1)S(1)} %copy.63, bf16[2,1,512]{1,2,0:T(8,128)(2,1)S(1)} %copy.64, bf16[2,13,512]{1,2,0:T(8,128)(2,1)S(1)} %broadcast_in_dim.15), dimensions={1} | concatenate | bytes 1114112 | tf_op jit(solution)/shard_map/concatenate | solution.py:212
  6.2 0.3 copy.65
  6.5 2.2 %collective-permute-start = (bf16[2,272,512]{2,1,0:T(8,128)(2,1)S(1)}, bf16[2,272,512]{2,1,0:T(8,128)(2,1)S(1)}, u32[]{:S(2)}, u32[]{:S(2)}) collective-permute-start(bf16[2,272,512]{2,1,0:T(8,128)(2,1)S(1)} %copy.65), channel_id=1, source_target_pairs={{0,1},{1,2},{2,3},{3,0},{4,5},{5,6},{6,7},{7,4},{8,9},{9,10},{10,1... | collective-permute-start | bytes 1671176 | tf_op jit(solution)/shard_map/ppermute | solution.py:191
  8.7 2.6 %collective-permute-start.1 = (bf16[2,272,512]{2,1,0:T(8,128)(2,1)S(1)}, bf16[2,272,512]{2,1,0:T(8,128)(2,1)S(1)}, u32[]{:S(2)}, u32[]{:S(2)}) collective-permute-start(bf16[2,272,512]{2,1,0:T(8,128)(2,1)S(1)} %copy.65), channel_id=1, source_target_pairs={{0,2},{1,3},{2,0},{3,1},{4,6},{5,7},{6,4},{7,5},{8,10},{9,11},{10,... | collective-permute-start | bytes 1671176 | tf_op jit(solution)/shard_map/ppermute | solution.py:191
  11.3 1.1 collective-permute-start.2
  12.4 9.9 %collective-permute-done = bf16[2,272,512]{2,1,0:T(8,128)(2,1)S(1)} collective-permute-done((bf16[2,272,512]{2,1,0:T(8,128)(2,1)S(1)}, bf16[2,272,512]{2,1,0:T(8,128)(2,1)S(1)}, u32[]{:S(2)}, u32[]{:S(2)}) %collective-permute-start) | collective-permute-done | bytes 557088 | tf_op jit(solution)/shard_map/ppermute | solution.py:191
  22.3 1.2 copy.66
  23.5 11.8 %collective-permute-done.1 = bf16[2,272,512]{2,1,0:T(8,128)(2,1)S(1)} collective-permute-done((bf16[2,272,512]{2,1,0:T(8,128)(2,1)S(1)}, bf16[2,272,512]{2,1,0:T(8,128)(2,1)S(1)}, u32[]{:S(2)}, u32[]{:S(2)}) %collective-permute-start.1) | collective-permute-done | bytes 557088 | tf_op jit(solution)/shard_map/ppermute | solution.py:191
  35.3 1.2 copy.68
  36.4 1.2 copy.70
  37.6 3.4 %fusion.15 = (bf16[4,1,2,272,512]{3,4,2,0,1:T(8,128)(2,1)S(1)}, bf16[4,2,272,512]{2,3,1,0:T(8,128)(2,1)}) fusion(bf16[1,2,272,512]{2,3,1,0:T(8,128)(2,1)} %bitcast.93, bf16[1,2,272,512]{2,3,1,0:T(8,128)(2,1)} %bitcast.92, bf16[1,2,272,512]{2,3,1,0:T(8,128)(2,1)} %bitcast.91, bf16[1,2,272,512]{2,3,1,0:T(8,128)(2,1)} %bitcast.89), kind=kLoop, calls=%fused_computation.57 | loop fusion | flops 3342336 | bytes 6684672 | tf_op jit(solution)/shard_map/stack | solution.py:221
  41.0 4.4 %copy.71 = bf16[4,2,272,512]{3,2,1,0:T(8,128)(2,1)} copy(bf16[4,2,272,512]{2,3,1,0:T(8,128)(2,1)} %get-tuple-element.12) | data formatting | bytes 4456448 | tf_op jit(solution)/shard_map/stack | solution.py:219
  45.5 1.5 collective-permute-start.3
  47.0 1.1 tile.2
  48.1 7.6 %all-to-all-start = ((bf16[16,128,256]{2,1,0:T(8,128)(2,1)}), bf16[16,128,256]{2,1,0:T(8,128)(2,1)}, u32[]{:S(2)}, u32[]{:S(2)}) async-start(bf16[16,128,256]{2,1,0:T(8,128)(2,1)} %tile.2), calls=%async_computation | async-start | bytes 2097152 | tf_op jit(solution)/shard_map/all_to_all | solution.py:215
  55.9 0.2 reshape.124
  56.1 0.1 le.16.qp_ref
  56.3 0.1 lt.84
  56.4 0.1 convert_reduce_fusion.1.rank_ref
  56.5 0.6 select_reduce_fusion.place_ref
  57.1 0.7 convert_reduce_fusion.2.n_ref
  57.8 16.0 %all-to-all-done = bf16[16,128,256]{2,1,0:T(8,128)(2,1)} async-done(((bf16[16,128,256]{2,1,0:T(8,128)(2,1)}), bf16[16,128,256]{2,1,0:T(8,128)(2,1)}, u32[]{:S(2)}, u32[]{:S(2)}) %all-to-all-start) | async-done | bytes 1048608 | tf_op jit(solution)/shard_map/all_to_all | solution.py:215
  73.8 2.3 %fusion.18 = (bf16[2048,128]{1,0:T(8,128)(2,1)}, bf16[2048,128]{1,0:T(8,128)(2,1)}) fusion(bf16[2048,256]{1,0:T(8,128)(2,1)} %bitcast.24), kind=kLoop, calls=%fused_computation.60 | loop fusion | bytes 2097152 | tf_op jit(solution)/shard_map/slice | solution.py:216
  76.1 4.6 %copy.72 = bf16[4,2,272,512]{2,3,1,0:T(8,128)(2,1)} copy(bf16[4,2,272,512]{3,2,1,0:T(8,128)(2,1)} %collective-permute-done.3) | data formatting | bytes 4456448 | tf_op jit(solution)/shard_map/ppermute | solution.py:191
  80.6 5.8 %pad_maximum_fusion = bf16[4,2,2,272,512]{3,4,2,0,1:T(8,128)(2,1)} fusion(bf16[4,1,2,272,512]{3,4,2,0,1:T(8,128)(2,1)} %bitcast.88, bf16[4,1,2,272,512]{3,4,2,0,1:T(8,128)(2,1)S(1)} %get-tuple-element.11), kind=kLoop, calls=%fused_computation | loop fusion | flops 2228224 | bytes 8912896 | tf_op jit(solution)/shard_map/stack | solution.py:221
  86.4 8.0 %copy.73 = bf16[4,2,2,272,512]{4,3,2,1,0:T(8,128)(2,1)} copy(bf16[4,2,2,272,512]{3,4,2,0,1:T(8,128)(2,1)} %pad_maximum_fusion) | data formatting | bytes 8912896 | tf_op jit(solution)/shard_map/stack | solution.py:221
  94.4 24.6 %local_lse.1 = f32[16,1,512]{2,1,0:T(1,128)} custom-call(s32[32]{0:T(128)} %copy-done.6, s32[32]{0:T(128)} %select_reduce_fusion.place_ref, s32[16]{0:T(128)} %convert_reduce_fusion.2.n_ref, s32[16]{0:T(128)} %copy-done.5, bf16[16,272,512]{2,1,0:T(8,128)(2,1)} %bitcast.86, bf16[2048,128]{1,0:T(8,128)(2,1)} %get-tuple-element.17.k_ref), custom_call_target="tpu_custom_call" | custom-call | tf_op jit(solution)/shard_map/local_lse/pallas_call | solution.py:101
  119.0 0.8 reduce.1
  119.9 0.1 collective-permute-start.4
  120.0 1.2 collective-permute-done.4
  121.2 0.1 multiply_add_fusion.1
  121.2 1.8 collective-permute-start.5
  123.1 0.1 collective-permute-start.7
  123.2 1.7 collective-permute-start.6
  124.9 2.2 %collective-permute-done.7 = f32[4,2,2,512]{3,2,1,0:T(2,128)S(1)} collective-permute-done((f32[4,2,2,512]{3,2,1,0:T(2,128)S(1)}, f32[4,2,2,512]{3,2,1,0:T(2,128)S(1)}, u32[]{:S(2)}, u32[]{:S(2)}) %collective-permute-start.7) | collective-permute-done | bytes 32800 | tf_op jit(solution)/shard_map/ppermute | solution.py:191
  127.0 0.4 collective-permute-done.6
  127.4 0.1 multiply_add_fusion
  127.6 0.7 reshape.133.lse_ref
  128.2 46.8 %local_grads.1 = (f32[16,128,512]{2,1,0:T(8,128)}, bf16[2048,256]{1,0:T(8,128)(2,1)}) custom-call(s32[32]{0:T(128)} %copy-done.6, s32[32]{0:T(128)} %select_reduce_fusion.place_ref, s32[16]{0:T(128)} %convert_reduce_fusion.2.n_ref, s32[16]{0:T(128)} %copy-done.5, bf16[16,272,512]{2,1,0:T(8,128)(2,1)} %bitcast.87, f32[16,1,512]{2,1,0:T(1,128)} %reshape.133.lse_ref, ...), custom_call_target="tpu_custom_call" | custom-call | tf_op jit(solution)/shard_map/local_grads/pallas_call | solution.py:167
  175.1 4.2 %fusion.17 = (f32[4,1,2,128,512]{4,3,2,1,0:T(8,128)}, f32[4,1,2,128,512]{4,3,2,1,0:T(8,128)S(1)}) fusion(f32[4,2,2,128,512]{4,3,2,1,0:T(8,128)} %bitcast.90), kind=kLoop, calls=%fused_computation.59 | loop fusion | bytes 8388608 | tf_op jit(solution)/shard_map/slice | solution.py:249
  179.2 1.8 copy.79
  181.1 9.5 %all-to-all-start.1 = ((bf16[16,128,256]{2,1,0:T(8,128)(2,1)}), bf16[16,128,256]{2,1,0:T(8,128)(2,1)S(1)}, u32[]{:S(2)}, u32[]{:S(2)}) async-start(bf16[16,128,256]{2,1,0:T(8,128)(2,1)} %bitcast.98), calls=%async_computation.1 | async-start | bytes 2097152 | tf_op jit(solution)/shard_map/all_to_all | solution.py:255
  190.6 1.9 copy.78
  192.5 3.2 %fusion.16 = (bf16[4,2,128,512]{2,3,1,0:T(8,128)(2,1)S(1)}, f32[4,2,128,512]{2,3,1,0:T(8,128)}) fusion(f32[4,2,128,512]{2,3,1,0:T(8,128)} %collective-permute-done.8, f32[4,1,2,128,512]{3,4,2,0,1:T(8,128)S(1)} %copy.78), kind=kLoop, calls=%fused_computation.58 | loop fusion | flops 1048576 | bytes 7340032 | tf_op jit(solution)/shard_map/convert.2
  195.7 0.1 slice_bitcast_fusion.3
  195.8 0.1 collective-permute-start.10
  195.9 4.4 %collective-permute-start.11 = (bf16[2,128,512]{1,2,0:T(8,128)(2,1)S(1)}, bf16[2,128,512]{1,2,0:T(8,128)(2,1)S(1)}, u32[]{:S(2)}, u32[]{:S(2)}) collective-permute-start(bf16[2,128,512]{1,2,0:T(8,128)(2,1)S(1)} %get-tuple-element.14), channel_id=1, source_target_pairs={{0,1},{1,2},{2,3},{3,0},{4,5},{5,6},{6,7},{7,4},{8,9},{9,10},{10,1... | collective-permute-start | bytes 786440 | tf_op jit(solution)/shard_map/ppermute | solution.py:191
  200.2 2.3 %collective-permute-start.9 = (bf16[2,128,512]{1,2,0:T(8,128)(2,1)S(1)}, bf16[2,128,512]{1,2,0:T(8,128)(2,1)S(1)}, u32[]{:S(2)}, u32[]{:S(2)}) collective-permute-start(bf16[2,128,512]{1,2,0:T(8,128)(2,1)S(1)} %get-tuple-element.13), channel_id=1, source_target_pairs={{0,3},{1,0},{2,1},{3,2},{4,7},{5,4},{6,5},{7,6},{8,11},{9,8},{10,9... | collective-permute-start | bytes 786440 | tf_op jit(solution)/shard_map/ppermute | solution.py:191
  202.6 5.1 %all-to-all-done.1 = bf16[16,128,256]{2,1,0:T(8,128)(2,1)S(1)} async-done(((bf16[16,128,256]{2,1,0:T(8,128)(2,1)}), bf16[16,128,256]{2,1,0:T(8,128)(2,1)S(1)}, u32[]{:S(2)}, u32[]{:S(2)}) %all-to-all-start.1) | async-done | bytes 1048608 | tf_op jit(solution)/shard_map/all_to_all | solution.py:255
  207.7 0.1 convert_reduce_fusion
  207.8 0.7 fusion.19
  208.5 2.8 %collective-permute-done.11 = bf16[2,128,512]{1,2,0:T(8,128)(2,1)S(1)} collective-permute-done((bf16[2,128,512]{1,2,0:T(8,128)(2,1)S(1)}, bf16[2,128,512]{1,2,0:T(8,128)(2,1)S(1)}, u32[]{:S(2)}, u32[]{:S(2)}) %collective-permute-start.11) | collective-permute-done | bytes 262176 | tf_op jit(solution)/shard_map/ppermute | solution.py:191
  211.2 0.8 collective-permute-done.9
  212.0 1.2 fusion.3
  213.2 0.2 copy.76
  213.3 0.8 copy.85
  (42 shorter events, 0.4 us)
Async XLA Ops:
  0.6 2.4 %copy-start.1 = (bf16[128,1024]{1,0:T(8,128)(2,1)S(1)}, bf16[128,1024]{1,0:T(8,128)(2,1)}, u32[]{:S(2)}) copy-start(bf16[128,1024]{1,0:T(8,128)(2,1)} %param.10) | copy-start | bytes 786436
  0.6 2.3 %copy-start.2 = (bf16[128,1024]{1,0:T(8,128)(2,1)S(1)}, bf16[128,1024]{1,0:T(8,128)(2,1)}, u32[]{:S(2)}) copy-start(bf16[128,1024]{1,0:T(8,128)(2,1)} %param.6) | copy-start | bytes 786436
  6.2 31.4 %copy-start = (bf16[2,272,512]{1,2,0:T(8,128)(2,1)}, bf16[2,272,512]{1,2,0:T(8,128)(2,1)S(1)}, u32[]{:S(2)}) copy-start(bf16[2,272,512]{1,2,0:T(8,128)(2,1)S(1)} %concatenate.21) | copy-start | bytes 1671172
  6.5 15.8 %collective-permute-start = (bf16[2,272,512]{2,1,0:T(8,128)(2,1)S(1)}, bf16[2,272,512]{2,1,0:T(8,128)(2,1)S(1)}, u32[]{:S(2)}, u32[]{:S(2)}) collective-permute-start(bf16[2,272,512]{2,1,0:T(8,128)(2,1)S(1)} %copy.65), channel_id=1, source_target_pairs={{0,1},{1,2},{2,3},{3,0},{4,5},{5,6},{6,7},{7,4},{8,9},{9,10},{10,1... | collective-permute-start | bytes 1671176 | tf_op jit(solution)/shard_map/ppermute | solution.py:191
  8.7 26.6 %collective-permute-start.1 = (bf16[2,272,512]{2,1,0:T(8,128)(2,1)S(1)}, bf16[2,272,512]{2,1,0:T(8,128)(2,1)S(1)}, u32[]{:S(2)}, u32[]{:S(2)}) collective-permute-start(bf16[2,272,512]{2,1,0:T(8,128)(2,1)S(1)} %copy.65), channel_id=1, source_target_pairs={{0,2},{1,3},{2,0},{3,1},{4,6},{5,7},{6,4},{7,5},{8,10},{9,11},{10,... | collective-permute-start | bytes 1671176 | tf_op jit(solution)/shard_map/ppermute | solution.py:191
  11.3 25.1 %collective-permute-start.2 = (bf16[2,272,512]{2,1,0:T(8,128)(2,1)S(1)}, bf16[2,272,512]{2,1,0:T(8,128)(2,1)S(1)}, u32[]{:S(2)}, u32[]{:S(2)}) collective-permute-start(bf16[2,272,512]{2,1,0:T(8,128)(2,1)S(1)} %copy.65), channel_id=1, source_target_pairs={{0,3},{1,0},{2,1},{3,2},{4,7},{5,4},{6,5},{7,6},{8,11},{9,8},{10,9... | collective-permute-start | bytes 1671176 | tf_op jit(solution)/shard_map/ppermute | solution.py:191
  41.0 6.0 %copy-start.3 = (bf16[128,128]{1,0:T(8,128)(2,1)S(1)}, bf16[128,128]{1,0:T(8,128)(2,1)}, u32[]{:S(2)}) copy-start(bf16[128,128]{1,0:T(8,128)(2,1)} %param.8) | copy-start | bytes 98308
  41.0 6.0 %copy-start.4 = (bf16[128,128]{1,0:T(8,128)(2,1)S(1)}, bf16[128,128]{1,0:T(8,128)(2,1)}, u32[]{:S(2)}) copy-start(bf16[128,128]{1,0:T(8,128)(2,1)} %param.7) | copy-start | bytes 98308
  41.0 14.9 %copy-start.7 = (s32[256]{0:T(256)S(1)}, s32[256]{0:T(256)}, u32[]{:S(2)}) copy-start(s32[256]{0:T(256)} %param.11) | copy-start | bytes 3076
  45.5 30.6 %collective-permute-start.3 = (bf16[4,2,272,512]{3,2,1,0:T(8,128)(2,1)}, bf16[4,2,272,512]{3,2,1,0:T(8,128)(2,1)}, u32[]{:S(2)}, u32[]{:S(2)}) collective-permute-start(bf16[4,2,272,512]{3,2,1,0:T(8,128)(2,1)} %copy.71), channel_id=1, source_target_pairs={{0,8},{8,0},{1,9},{9,1},{2,10},{10,2},{3,11},{11,3},{4,12},{12,4},... | collective-permute-start | bytes 6684680 | tf_op jit(solution)/shard_map/ppermute | solution.py:191
  48.1 25.7 %all-to-all-start = ((bf16[16,128,256]{2,1,0:T(8,128)(2,1)}), bf16[16,128,256]{2,1,0:T(8,128)(2,1)}, u32[]{:S(2)}, u32[]{:S(2)}) async-start(bf16[16,128,256]{2,1,0:T(8,128)(2,1)} %tile.2), calls=%async_computation | async-start | bytes 2097152 | tf_op jit(solution)/shard_map/all_to_all | solution.py:215
  56.2 24.4 %copy-start.5 = (s32[16]{0:T(128)}, s32[16]{0:T(128)S(1)}, u32[]{:S(2)}) copy-start(s32[16]{0:T(128)S(1)} %le.16.qp_ref) | copy-start | bytes 196
  56.5 24.2 %copy-start.6 = (s32[32]{0:T(128)}, s32[32]{0:T(128)S(1)}, u32[]{:S(2)}) copy-start(s32[32]{0:T(128)S(1)} %convert_reduce_fusion.1.rank_ref) | copy-start | bytes 388
  119.9 1.3 collective-permute-start.4
  121.2 3.6 %collective-permute-start.5 = (f32[4,2,2,512]{3,2,1,0:T(2,128)S(1)}, f32[4,2,2,512]{3,2,1,0:T(2,128)S(1)}, u32[]{:S(2)}, u32[]{:S(2)}) collective-permute-start(f32[4,2,2,512]{3,2,1,0:T(2,128)S(1)} %multiply_add_fusion.1), channel_id=1, source_target_pairs={{0,3},{1,0},{2,1},{3,2},{4,7},{5,4},{6,5},{7,6},{8,11},{9,8},{10,9... | collective-permute-start | bytes 98312 | tf_op jit(solution)/shard_map/ppermute | solution.py:191
  123.1 4.0 %collective-permute-start.7 = (f32[4,2,2,512]{3,2,1,0:T(2,128)S(1)}, f32[4,2,2,512]{3,2,1,0:T(2,128)S(1)}, u32[]{:S(2)}, u32[]{:S(2)}) collective-permute-start(f32[4,2,2,512]{3,2,1,0:T(2,128)S(1)} %multiply_add_fusion.1), channel_id=1, source_target_pairs={{0,1},{1,2},{2,3},{3,0},{4,5},{5,6},{6,7},{7,4},{8,9},{9,10},{10,1... | collective-permute-start | bytes 98312 | tf_op jit(solution)/shard_map/ppermute | solution.py:191
  123.2 4.3 %collective-permute-start.6 = (f32[4,2,2,512]{3,2,1,0:T(2,128)S(1)}, f32[4,2,2,512]{3,2,1,0:T(2,128)S(1)}, u32[]{:S(2)}, u32[]{:S(2)}) collective-permute-start(f32[4,2,2,512]{3,2,1,0:T(2,128)S(1)} %multiply_add_fusion.1), channel_id=1, source_target_pairs={{0,2},{1,3},{2,0},{3,1},{4,6},{5,7},{6,4},{7,5},{8,10},{9,11},{10,... | collective-permute-start | bytes 98312 | tf_op jit(solution)/shard_map/ppermute | solution.py:191
  181.1 11.4 %collective-permute-start.8 = (f32[4,2,128,512]{2,3,1,0:T(8,128)}, f32[4,2,128,512]{2,3,1,0:T(8,128)}, u32[]{:S(2)}, u32[]{:S(2)}) collective-permute-start(f32[4,2,128,512]{2,3,1,0:T(8,128)} %bitcast.94), channel_id=1, source_target_pairs={{0,8},{8,0},{1,9},{9,1},{2,10},{10,2},{3,11},{11,3},{4,12},{12,4},... | collective-permute-start | bytes 6291464 | tf_op jit(solution)/shard_map/ppermute | solution.py:191
  181.1 26.6 %all-to-all-start.1 = ((bf16[16,128,256]{2,1,0:T(8,128)(2,1)}), bf16[16,128,256]{2,1,0:T(8,128)(2,1)S(1)}, u32[]{:S(2)}, u32[]{:S(2)}) async-start(bf16[16,128,256]{2,1,0:T(8,128)(2,1)} %bitcast.98), calls=%async_computation.1 | async-start | bytes 2097152 | tf_op jit(solution)/shard_map/all_to_all | solution.py:255
  195.8 12.7 %collective-permute-start.10 = (bf16[2,128,512]{1,2,0:T(8,128)(2,1)S(1)}, bf16[2,128,512]{1,2,0:T(8,128)(2,1)S(1)}, u32[]{:S(2)}, u32[]{:S(2)}) collective-permute-start(bf16[2,128,512]{1,2,0:T(8,128)(2,1)S(1)} %get-tuple-element.15), channel_id=1, source_target_pairs={{0,2},{1,3},{2,0},{3,1},{4,6},{5,7},{6,4},{7,5},{8,10},{9,11},{10,... | collective-permute-start | bytes 786440 | tf_op jit(solution)/shard_map/ppermute | solution.py:191
  195.9 15.4 %collective-permute-start.11 = (bf16[2,128,512]{1,2,0:T(8,128)(2,1)S(1)}, bf16[2,128,512]{1,2,0:T(8,128)(2,1)S(1)}, u32[]{:S(2)}, u32[]{:S(2)}) collective-permute-start(bf16[2,128,512]{1,2,0:T(8,128)(2,1)S(1)} %get-tuple-element.14), channel_id=1, source_target_pairs={{0,1},{1,2},{2,3},{3,0},{4,5},{5,6},{6,7},{7,4},{8,9},{9,10},{10,1... | collective-permute-start | bytes 786440 | tf_op jit(solution)/shard_map/ppermute | solution.py:191
  200.2 11.7 %collective-permute-start.9 = (bf16[2,128,512]{1,2,0:T(8,128)(2,1)S(1)}, bf16[2,128,512]{1,2,0:T(8,128)(2,1)S(1)}, u32[]{:S(2)}, u32[]{:S(2)}) collective-permute-start(bf16[2,128,512]{1,2,0:T(8,128)(2,1)S(1)} %get-tuple-element.13), channel_id=1, source_target_pairs={{0,3},{1,0},{2,1},{3,2},{4,7},{5,4},{6,5},{7,6},{8,11},{9,8},{10,9... | collective-permute-start | bytes 786440 | tf_op jit(solution)/shard_map/ppermute | solution.py:191

commit v2 on v1

v2 whole, which is shorter than its diff:
```python
import functools
import math

import jax
import jax.numpy as jnp
from jax import lax
from jax.experimental import pallas as pl
from jax.experimental.pallas import tpu as pltpu
from jax.sharding import Mesh, PartitionSpec as P

DH = 128
HEADS = 8
BLOCK = 64
ROWS = HEADS * BLOCK
MESSAGE = 2 * ROWS + 16
SCALE = DH ** -0.5
C2 = SCALE * math.log2(math.e)
NEG = -1e30
KB = 4
KT = KB * BLOCK
UNROLL = 4
HALVES = 1
VMEM_LIMIT = 56 * 1024 * 1024
F32 = jnp.float32
BF16 = jnp.bfloat16
KEY_AXES = ("x", "zl", "zh")
SMEM = pl.BlockSpec(memory_space=pltpu.SMEM)
VMEM = pl.BlockSpec(memory_space=pltpu.VMEM)


def nn(a, b):
    return lax.dot_general(a, b, (((1,), (0,)), ((), ())), preferred_element_type=F32)


def nt(a, b):
    return lax.dot_general(a, b, (((1,), (1,)), ((), ())), preferred_element_type=F32)


def params():
    return pltpu.CompilerParams(vmem_limit_bytes=VMEM_LIMIT)


def cost(products, nq, count):
    area = nq * ROWS * count // 2
    return pl.CostEstimate(flops=products * 4 * area * DH, bytes_accessed=8 << 20, transcendentals=area)


def message_kernel(q_ref, g_ref, o_ref, *out_refs):
    for blk in range(2):
        out_ref, at = out_refs[blk * HALVES // 2], blk % (2 // HALVES)
        tokens = slice(blk * BLOCK, (blk + 1) * BLOCK)
        parts = []
        for h in range(HEADS):
            lanes = slice(h * DH, (h + 1) * DH)
            g = g_ref[tokens, lanes]
            out_ref[at, h * BLOCK:(h + 1) * BLOCK, :] = q_ref[tokens, lanes]
            out_ref[at, ROWS + h * BLOCK:ROWS + (h + 1) * BLOCK, :] = g
            parts.append(g.astype(F32) * o_ref[tokens, lanes].astype(F32))
        delta = jnp.sum(jnp.concatenate(parts, 0).T, axis=0, keepdims=True)
        rows = []
        rest = delta
        for _ in range(3):
            part = rest.astype(BF16).astype(F32)
            rest = rest - part
            rows += [part[:, c * DH:(c + 1) * DH] for c in range(ROWS // DH)]
        rows.append(jnp.zeros((16 - len(rows), DH), F32))
        out_ref[at, 2 * ROWS:, :] = jnp.concatenate(rows, 0).astype(BF16)


def make_messages(queries, out_grad, outputs):
    shape = jax.ShapeDtypeStruct((2 // HALVES, MESSAGE, DH), BF16)
    return pl.pallas_call(
        message_kernel,
        out_shape=(shape,) * HALVES,
        in_specs=[VMEM] * 3,
        out_specs=(VMEM,) * HALVES,
        compiler_params=params(),
        name="make_messages",
    )(queries, out_grad, outputs)


def finish_kernel(*refs):
    out_ref = refs[-1]
    for blk in range(2):
        per_half = 2 // HALVES
        half, at = blk // per_half, blk % per_half
        own, *others = refs[half * 4:half * 4 + 4]
        total = own[at]
        for other in others:
            total = total + other[at].astype(F32)
        total = total.T.astype(BF16)
        for h in range(HEADS):
            out_ref[blk * BLOCK:(blk + 1) * BLOCK, h * DH:(h + 1) * DH] = total[h * BLOCK:(h + 1) * BLOCK]


def finish_queries(parts):
    return pl.pallas_call(
        finish_kernel,
        out_shape=jax.ShapeDtypeStruct((2 * BLOCK, HEADS * DH), BF16),
        in_specs=[VMEM] * len(parts),
        out_specs=VMEM,
        compiler_params=params(),
        name="finish_queries",
    )(*parts)


def sort_blocks(rank_ref, src, lanes, dst, nk):
    def body(j, c):
        r = pl.multiple_of(rank_ref[j] * BLOCK, BLOCK)
        dst[pl.ds(r, BLOCK), :] = src[pl.ds(pl.multiple_of(j * BLOCK, BLOCK), BLOCK), lanes]
        return c

    lax.fori_loop(0, nk, body, 0, unroll=4)


def fill_work(n_ref, qp_ref, wb, wt, wq, nq):
    wb[0] = 0
    wt[0] = 0
    wq[0] = -1

    def block(b, w):
        count = (n_ref[b] + KB - 1) // KB

        def tile(t, c):
            wb[w + t] = b
            wt[w + t] = t
            wq[w + t] = qp_ref[b]
            return c

        lax.fori_loop(0, count, tile, 0)
        return w + count

    end = lax.fori_loop(0, nq, block, 1)
    for i in range(UNROLL + 1):
        wb[end + i] = 0
        wt[end + i] = 0
        wq[end + i] = -1
    return end


def run_work(end, prepare, use):
    def body(i, c):
        for u in range(UNROLL):
            w = i * UNROLL + u
            prepare(w + 1, (u + 1) % 2)
            use(w, u % 2)
        return c

    lax.fori_loop(0, (end + UNROLL - 1) // UNROLL, body, 0)


def work_scratch(nq, nk):
    size = nq * ((nk + KB - 1) // KB) + UNROLL + 2
    return [pltpu.SMEM((size,), jnp.int32)] * 3


def difference():
    key = lax.broadcasted_iota(jnp.int32, (BLOCK, ROWS), 0)
    query = lax.broadcasted_iota(jnp.int32, (BLOCK, ROWS), 1) % BLOCK
    return key - query


def causal(s, place_ref, t, query_place, diff):
    parts = []
    for u in range(KB):
        place = place_ref[t * KB + u]
        limit = jnp.where(place < query_place, BLOCK, jnp.where(place == query_place, 0, -2 * BLOCK))
        parts.append(jnp.where(diff <= limit, s[u * BLOCK:(u + 1) * BLOCK], NEG))
    return jnp.concatenate(parts, 0)


def lse_kernel(nq, nk, rank_ref, place_ref, n_ref, qp_ref, *refs):
    pieces, (kv_ref, lse_ref, q_all, ks, s_buf, diff, l8, m8, wb, wt, wq) = refs[:8], refs[8:]
    per = nq // 8
    for i, piece in enumerate(pieces):
        q_all[i * per:(i + 1) * per] = piece[:, :ROWS, :]
    sort_blocks(rank_ref, kv_ref, slice(0, DH), ks, nk)
    diff[...] = difference()
    l8[...] = jnp.zeros_like(l8)
    end = fill_work(n_ref, qp_ref, wb, wt, wq, nq)

    def prepare(w, slot):
        keys = ks[pl.ds(pl.multiple_of(wt[w] * KT, KT), KT), :]
        s_buf[slot] = nt(keys, q_all[wb[w]])

    def use(w, slot):
        s = causal(s_buf[slot] * C2, place_ref, wt[w], wq[w], diff[...])
        l8[wb[w]] += jnp.sum(jnp.exp2(s).reshape(KT // 8, 8, ROWS), axis=0)

    run_work(end, prepare, use)
    fine = jnp.ones((1, ROWS), F32)
    for b in range(nq):
        total = jnp.sum(l8[b], axis=0, keepdims=True)
        seen = n_ref[b] > 0
        inside = jnp.where((total > 1e-18) & (total < 1e30), 1.0, 0.0)
        fine = jnp.minimum(fine, jnp.where(seen, inside, 1.0))
        lse_ref[b] = jnp.where(seen, jnp.log2(total), NEG)

    @pl.when(jnp.min(fine) < 0.5)
    def _():
        def block(b, c):
            m8[...] = jnp.full_like(m8, 0.5 * NEG)
            l8[0] = jnp.zeros((8, ROWS), F32)

            def tile(t, c):
                keys = ks[pl.ds(pl.multiple_of(t * KT, KT), KT), :]
                s = causal(nt(keys, q_all[b]) * C2, place_ref, t, qp_ref[b], diff[...])
                s = s.reshape(KT // 8, 8, ROWS)
                m = m8[...]
                top = jnp.maximum(m, jnp.max(s, axis=0))
                l8[0] = l8[0] * jnp.exp2(m - top) + jnp.sum(jnp.exp2(s - top[None]), axis=0)
                m8[...] = top
                return c

            lax.fori_loop(0, (n_ref[b] + KB - 1) // KB, tile, 0)
            m = m8[...]
            top = jnp.max(m, axis=0, keepdims=True)
            total = jnp.sum(l8[0] * jnp.exp2(m - top), axis=0, keepdims=True)
            lse_ref[b] = jnp.where(n_ref[b] > 0, top + jnp.log2(total), NEG)
            return c

        lax.fori_loop(0, nq, block, 0)


def local_lse(scalars, pieces, kv):
    nq = 8 * pieces[0].shape[0]
    count = kv.shape[0]
    nk = count // BLOCK
    return pl.pallas_call(
        functools.partial(lse_kernel, nq, nk),
        out_shape=jax.ShapeDtypeStruct((nq, 1, ROWS), F32),
        in_specs=[SMEM] * 4 + [VMEM] * 9,
        out_specs=VMEM,
        scratch_shapes=[
            pltpu.VMEM((nq, ROWS, DH), BF16),
            pltpu.VMEM((count, DH), BF16),
            pltpu.VMEM((2, KT, ROWS), F32),
            pltpu.VMEM((BLOCK, ROWS), jnp.int32),
            pltpu.VMEM((nq, 8, ROWS), F32),
            pltpu.VMEM((8, ROWS), F32),
        ]
        + work_scratch(nq, nk),
        compiler_params=params(),
        cost_estimate=cost(1, nq, count),
        name="local_lse",
    )(*scalars, *pieces, kv)


def grad_kernel(nq, nk, first, last, rank_ref, place_ref, n_ref, qp_ref, *refs):
    pieces, refs = refs[:8], refs[8:]
    lse_ref, kv_ref, refs = refs[0], refs[1], refs[2:]
    if not first:
        sums_in, refs = refs[0], refs[1:]
    keep_ref, send_ref, kv_out, refs = refs[0], refs[1], refs[2], refs[3:]
    qg, delta, ks, vs, kst, sums, dqa, s_buf, dp_buf, diff, wb, wt, wq = refs
    per = nq // 8
    for i, piece in enumerate(pieces):
        for j in range(per):
            b = i * per + j
            qg[b] = piece[j, :2 * ROWS, :]
            tail = piece[j, 2 * ROWS:, :].astype(F32)
            n = ROWS // DH
            tail = tail[0:n] + tail[n:2 * n] + tail[2 * n:3 * n]
            for c in range(n):
                delta[b, :, c * DH:(c + 1) * DH] = tail[c:c + 1]
    sort_blocks(rank_ref, kv_ref, slice(0, DH), ks, nk)
    sort_blocks(rank_ref, kv_ref, slice(DH, 2 * DH), vs, nk)
    kst[...] = ks[...].T
    sums[...] = jnp.zeros_like(sums) if first else sums_in[...]
    dqa[...] = jnp.zeros_like(dqa)
    s_buf[0] = jnp.zeros((KT, ROWS), F32)
    dp_buf[0] = jnp.zeros((KT, ROWS), F32)
    diff[...] = difference()
    end = fill_work(n_ref, qp_ref, wb, wt, wq, nq)

    def prepare(w, slot):
        at = pl.ds(pl.multiple_of(wt[w] * KT, KT), KT)
        b = wb[w]
        s_buf[slot] = nt(ks[at, :], qg[b, :ROWS, :])
        dp_buf[slot] = nt(vs[at, :], qg[b, ROWS:, :])

    def use(w, slot):
        at = pl.ds(pl.multiple_of(wt[w] * KT, KT), KT)
        b = wb[w]
        p = jnp.exp2(causal(s_buf[slot] * C2 - lse_ref[b], place_ref, wt[w], wq[w], diff[...]))
        ds = (p * (dp_buf[slot] - delta[b])).astype(BF16)
        sums[1, at, :] += nn(p.astype(BF16), qg[b, ROWS:, :])
        sums[0, at, :] += nn(ds, qg[b, :ROWS, :])
        dqa[b] += nn(kst[:, at], ds)

    run_work(end, prepare, use)
    for i in range(4):
        for j in range(per):
            keep_ref[i, j] = dqa[2 * i * per + j] * SCALE
            send_ref[i, j] = dqa[(2 * i + 1) * per + j] * SCALE
    if not last:
        kv_out[...] = sums[...]
        return

    def body(j, c):
        r = pl.ds(pl.multiple_of(rank_ref[j] * BLOCK, BLOCK), BLOCK)
        at = pl.ds(pl.multiple_of(j * BLOCK, BLOCK), BLOCK)
        kv_out[at, :DH] = (sums[0, r, :] * SCALE).astype(BF16)
        kv_out[at, DH:] = sums[1, r, :].astype(BF16)
        return c

    lax.fori_loop(0, nk, body, 0, unroll=2)


def local_grads(scalars, pieces, lse, kv, sums, last):
    nq = 8 * pieces[0].shape[0]
    count = kv.shape[0]
    nk = count // BLOCK
    first = sums is None
    query_shape = jax.ShapeDtypeStruct((4, nq // 8, DH, ROWS), F32)
    if last:
        kv_shape = jax.ShapeDtypeStruct((count, 2 * DH), BF16)
    else:
        kv_shape = jax.ShapeDtypeStruct((2, count, DH), F32)
    return pl.pallas_call(
        functools.partial(grad_kernel, nq, nk, first, last),
        out_shape=(query_shape, query_shape, kv_shape),
        in_specs=[SMEM] * 4 + [VMEM] * (10 if first else 11),
        out_specs=(VMEM,) * 3,
        scratch_shapes=[
            pltpu.VMEM((nq, 2 * ROWS, DH), BF16),
            pltpu.VMEM((nq, 1, ROWS), F32),
            pltpu.VMEM((count, DH), BF16),
            pltpu.VMEM((count, DH), BF16),
            pltpu.VMEM((DH, count), BF16),
            pltpu.VMEM((2, count, DH), F32),
            pltpu.VMEM((nq, DH, ROWS), F32),
            pltpu.VMEM((2, KT, ROWS), F32),
            pltpu.VMEM((2, KT, ROWS), F32),
            pltpu.VMEM((BLOCK, ROWS), jnp.int32),
        ]
        + work_scratch(nq, nk),
        compiler_params=params(),
        cost_estimate=cost(5, nq, count),
        name="local_grads",
    )(*scalars, *pieces, lse, kv, *(() if first else (sums,)))


def along(axis, shift, size, array):
    return lax.ppermute(array, axis, [(i, (i + shift) % size) for i in range(size)])


def combine(parts):
    top = functools.reduce(jnp.maximum, parts)
    return top + jnp.log2(sum(jnp.exp2(part - top) for part in parts))


def all_lse(part):
    shape = part.shape
    part = part.reshape(4, 2, -1, ROWS)
    part = combine([part, along("core", 1, 2, part)[:, ::-1]])
    around = [part] + [jnp.roll(along("y", -d, 4, part), -d, axis=0) for d in (1, 2, 3)]
    return combine(around).reshape(shape)


def shards(queries, keys, values, outputs, out_grad, block_order):
    x, zl, core, zh, y = (lax.axis_index(a) for a in ("x", "zl", "core", "zh", "y"))

    pair = jnp.concatenate([keys, values], axis=1)
    kv = lax.all_to_all(jnp.tile(pair, (16, 1)), KEY_AXES, 0, 0, tiled=True)

    halves = []
    for message in make_messages(queries, out_grad, outputs):
        pieces = [message] + [along("y", s, 4, message) for s in (1, 3, 2)]
        pieces = [pieces[i] for i in (0, 1, 3, 2)]
        halves.append([a for piece in pieces for a in (piece, along("core", 1, 2, piece))])

    order = block_order.reshape(4, 2, 2, 2, 4, 2)
    key_place = lax.dynamic_slice(order, (0, 0, core, 0, y, 0), (4, 2, 1, 2, 1, 2)).reshape(32)
    here = lax.dynamic_slice(order, (x, zl, 0, zh, 0, 0), (1, 1, 2, 1, 4, 2)).reshape(2, 4, 2)
    here = jnp.stack([jnp.stack([here[core ^ c, (y - s) % 4] for c in range(2)]) for s in range(4)])
    rank = jnp.sum(key_place[:, None] < key_place[None, :], axis=0, dtype=jnp.int32)
    spots = lax.broadcasted_iota(jnp.int32, (32, 32), 0)
    place = jnp.sum(jnp.where(rank[None, :] == spots, key_place[None, :], 0), axis=1, dtype=jnp.int32)
    per = 2 // HALVES
    scalars = []
    for half in range(HALVES):
        query_place = here[:, :, half * per:(half + 1) * per].reshape(8 * per)
        visible = jnp.sum(key_place[None, :] <= query_place[:, None], axis=1, dtype=jnp.int32)
        scalars.append((rank, place, visible, query_place))

    sums = [all_lse(local_lse(sc, pieces, kv)) for sc, pieces in zip(scalars, halves)]

    kv_part = None
    query_parts = []
    for half in range(HALVES):
        keep, send, kv_part = local_grads(
            scalars[half], halves[half], sums[half], kv, kv_part, half == HALVES - 1
        )
        part = keep + along("core", 1, 2, send)
        query_parts += [part[0]] + [along("y", -s, 4, part[s].astype(BF16)) for s in (1, 3, 2)]
    terms = lax.all_to_all(kv_part, KEY_AXES, 0, 0, tiled=True)
    kv_grad = jnp.sum(terms.astype(F32).reshape(16, 2 * BLOCK, 2 * DH), axis=0)
    return finish_queries(query_parts), kv_grad[:, :DH], kv_grad[:, DH:]


def solution(mesh):
    fine = Mesh(mesh.devices.reshape(4, 2, 2, 2, 4), ("x", "zl", "core", "zh", "y"))
    rows = P(("x", "zl", "core", "zh", "y"), None)
    return jax.shard_map(
        shards,
        mesh=fine,
        in_specs=(rows,) * 5 + (P(),),
        out_specs=(rows,) * 3,
        check_vma=False,
    )
```

time: 217 us -> 178 us (0.82)
  local copies, waits for them, and re-layouts: 38.8 us -> 5.96 us
  blocking collectives: 0 us -> 30 us
  waiting for transfers between devices: 50.1 us -> 28.8 us
  other arithmetic: 17.6 us -> 3.93 us
  starting transfers between devices: 35 us -> 22.3 us
  Pallas kernels: 71.5 us -> 83.9 us
    all_to_all x0 -> x1, blocking collectives: none -> 30 us  [shards(): terms = lax.all_to_all(kv_part, KEY_AXES, 0, 0, tiled=True)]
    all_to_all x2 -> x1, waiting for transfers between devices: 21.1 us -> 0.01 us  [shards(): kv = lax.all_to_all(jnp.tile(pair, (16, 1)), KEY_AXES, 0, 0, tiled=True)]
    another operation x6 -> x1, local copies, waits for them, and re-layouts: 14.1 us -> 1.08 us  [shards(): kv = lax.all_to_all(jnp.tile(pair, (16, 1)), KEY_AXES, 0, 0, tiled=True)]
    pallas_call x2 -> x4, Pallas kernels: 71.5 us -> 83.9 us  [the longest x1 40.9 us: local_lse(): pl.pallas_call(functools.partial(lse_kernel, nq, nk), out_shape=jax.Shape...]
    another operation x4 -> x1, other arithmetic: 12.4 us -> 0.51 us  [the longest x2 9.17 us: shards(): qg = jnp.stack([mine, other], axis=1).reshape(16, 2 * DH + 16, ROWS)]
    all_to_all x2 -> x1, starting transfers between devices: 17.1 us -> 7.6 us  [shards(): kv = lax.all_to_all(jnp.tile(pair, (16, 1)), KEY_AXES, 0, 0, tiled=True)]
    ppermute x4 -> x0, local copies, waits for them, and re-layouts: 8.08 us -> none  [along(): lax.ppermute(array, axis, [(i, (i + shift) % size) for i in range(size)])]
    slice x8 -> x6, local copies, waits for them, and re-layouts: 7.1 us -> 0.67 us  [the longest x1 0.66 us: shards(): return (finish_queries(query_parts), kv_grad[:, :DH], kv_grad[:, DH:])]
  transfers between devices with their start and end apart: 14 -> 16, of which waited for: 9 -> 8; matrix products, arithmetic and copies ran while one was open for 6% -> 3% of each run, Pallas kernels for 0% -> 0%
where the time goes in v2:
time: 178 us; the launch traced here: 176 us
  Pallas kernels  83.9 us (47%)
  blocking collectives  30 us (17%)
  waiting for transfers between devices  28.8 us (16%)
  starting transfers between devices  22.3 us (13%)
  local copies, waits for them, and re-layouts  5.96 us (3%)
  other arithmetic  3.93 us (2%)
    pallas_call x1, Pallas kernels, local_lse(): pl.pallas_call(functools.partial(lse_kernel, nq, nk), out_shape=jax.Shape...  40.9 us
    pallas_call x1, Pallas kernels, local_grads(): pl.pallas_call(functools.partial(grad_kernel, nq, nk, first, last), out_s...  38.7 us
    all_to_all x1, blocking collectives, shards(): terms = lax.all_to_all(kv_part, KEY_AXES, 0, 0, tiled=True)  30 us
    ppermute x15, waiting for transfers between devices, along(): lax.ppermute(array, axis, [(i, (i + shift) % size) for i in range(size)])  28.8 us
    ppermute x15, starting transfers between devices, along(): lax.ppermute(array, axis, [(i, (i + shift) % size) for i in range(size)])  14.7 us
    all_to_all x1, starting transfers between devices, shards(): kv = lax.all_to_all(jnp.tile(pair, (16, 1)), KEY_AXES, 0, 0, tiled=True)  7.6 us
  transfers between devices with their start and end apart: 16, of which 8 were waited for; matrix products, arithmetic and copies ran while one was open for 3% of the time, Pallas kernels for 0%

profile of v2, /device:TPU:1, one launch (start us, length us, event | category | flops | bytes accessed | tf_op | source)
XLA Modules:
  0.0 175.8 jit_solution(16271323820166773806)
XLA Ops:
  0.6 2.1 %make_messages.1.refs_0_ = bf16[2,1040,128]{2,1,0:T(8,128)(2,1)} custom-call(bf16[128,1024]{1,0:T(8,128)(2,1)} %q_ref.1, bf16[128,1024]{1,0:T(8,128)(2,1)} %g_ref.1, bf16[128,1024]{1,0:T(8,128)(2,1)} %o_ref.1), custom_call_target="tpu_custom_call" | custom-call | tf_op jit(solution)/shard_map/make_messages/pallas_call | solution.py:72
  2.8 3.6 %collective-permute-start.5 = (bf16[2,1040,128]{2,1,0:T(8,128)(2,1)}, bf16[2,1040,128]{2,1,0:T(8,128)(2,1)S(1)}, u32[]{:S(2)}, u32[]{:S(2)}) collective-permute-start(bf16[2,1040,128]{2,1,0:T(8,128)(2,1)} %make_messages.1.refs_0_), channel_id=1, source_target_pairs={{0,3},{1,0},{2,1},{3,2},{4,7},{5,4},{6,5},{7,6},{8,11},{9,8},{10,9... | collective-permute-start | bytes 1597448 | tf_op jit(solution)/shard_map/ppermute | solution.py:345
  6.3 0.3 collective-permute-start.3
  6.7 0.7 collective-permute-start.1
  7.4 0.8 pad_maximum_fusion
  8.2 1.1 tile.2
  9.2 7.6 %all-to-all-start = ((bf16[16,128,256]{2,1,0:T(8,128)(2,1)}), bf16[16,128,256]{2,1,0:T(8,128)(2,1)S(1)}, u32[]{:S(2)}, u32[]{:S(2)}) async-start(bf16[16,128,256]{2,1,0:T(8,128)(2,1)} %tile.2), calls=%async_computation | async-start | bytes 2097152 | tf_op jit(solution)/shard_map/all_to_all | solution.py:365
  16.9 0.0 copy-done.2
  16.9 1.9 %collective-permute-start = (bf16[2,1040,128]{2,1,0:T(8,128)(2,1)S(1)}, bf16[2,1040,128]{2,1,0:T(8,128)(2,1)}, u32[]{:S(2)}, u32[]{:S(2)}) collective-permute-start(bf16[2,1040,128]{2,1,0:T(8,128)(2,1)S(1)} %copy-done.2), channel_id=1, source_target_pairs={{0,8},{8,0},{1,9},{9,1},{2,10},{10,2},{3,11},{11,3},{4,12},{12,4},... | collective-permute-start | bytes 1597448 | tf_op jit(solution)/shard_map/ppermute | solution.py:345
  18.7 0.0 copy-done.6
  18.7 0.2 reshape.50
  19.0 0.1 lt.84
  19.1 9.6 %collective-permute-done.5.refs_6_ = bf16[2,1040,128]{2,1,0:T(8,128)(2,1)S(1)} collective-permute-done((bf16[2,1040,128]{2,1,0:T(8,128)(2,1)}, bf16[2,1040,128]{2,1,0:T(8,128)(2,1)S(1)}, u32[]{:S(2)}, u32[]{:S(2)}) %collective-permute-start.5) | collective-permute-done | bytes 532512 | tf_op jit(solution)/shard_map/ppermute | solution.py:345
  28.7 1.7 collective-permute-start.6
  30.4 0.0 collective-permute-done.3.refs_4_
  30.4 0.1 collective-permute-start.4
  30.5 3.0 %collective-permute-done.1.refs_2_ = bf16[2,1040,128]{2,1,0:T(8,128)(2,1)S(1)} collective-permute-done((bf16[2,1040,128]{2,1,0:T(8,128)(2,1)}, bf16[2,1040,128]{2,1,0:T(8,128)(2,1)S(1)}, u32[]{:S(2)}, u32[]{:S(2)}) %collective-permute-start.1) | collective-permute-done | bytes 532512 | tf_op jit(solution)/shard_map/ppermute | solution.py:345
  33.5 0.5 collective-permute-start.2
  34.0 0.1 le.16.qp_ref
  34.1 0.1 convert_reduce_fusion.1.rank_ref
  34.2 0.6 select_reduce_fusion.place_ref
  34.8 0.7 convert_reduce_fusion.2.n_ref
  35.5 0.0 collective-permute-done.refs_1_
  35.5 0.0 all-to-all-done
  35.5 0.0 collective-permute-done.6.refs_7_
  35.5 0.0 collective-permute-done.4.refs_5_
  35.5 0.1 collective-permute-done.2.refs_3_
  35.7 0.0 copy-done.8
  35.7 0.0 copy-done.9
  35.7 0.0 copy-done.10
  35.7 0.0 copy-done.7
  35.7 0.0 copy-done.11
  35.7 0.8 copy-done.1
  36.5 40.9 %local_lse.1 = f32[16,1,512]{2,1,0:T(1,128)} custom-call(s32[32]{0:T(128)} %copy-done.11, s32[32]{0:T(128)} %select_reduce_fusion.place_ref, s32[16]{0:T(128)} %convert_reduce_fusion.2.n_ref, s32[16]{0:T(128)} %copy-done.7, bf16[2,1040,128]{2,1,0:T(8,128)(2,1)} %make_messages.1.refs_0_, bf16[2,1040,128]{2,1,0:T(8,128)(2,1)} %collective-permute-done.refs_1_, ...), custom_call_target="tpu_custom_call" | custom-call | flops 4294967296 | bytes 8388608 | tf_op jit(solution)/shard_map/local_lse/pallas_call | solution.py:229
  77.4 0.8 reduce.1
  78.3 0.1 collective-permute-start.7
  78.4 1.2 collective-permute-done.7
  79.6 0.1 multiply_add_fusion.1
  79.7 0.1 collective-permute-start.10
  79.7 2.7 %collective-permute-start.8 = (f32[4,2,2,512]{3,2,1,0:T(2,128)S(1)}, f32[4,2,2,512]{3,2,1,0:T(2,128)S(1)}, u32[]{:S(2)}, u32[]{:S(2)}) collective-permute-start(f32[4,2,2,512]{3,2,1,0:T(2,128)S(1)} %multiply_add_fusion.1), channel_id=1, source_target_pairs={{0,3},{1,0},{2,1},{3,2},{4,7},{5,4},{6,5},{7,6},{8,11},{9,8},{10,9... | collective-permute-start | bytes 98312 | tf_op jit(solution)/shard_map/ppermute | solution.py:345
  82.4 0.0 collective-permute-start.9
  82.4 1.3 collective-permute-done.10
  83.7 0.0 collective-permute-done.8
  83.7 2.9 %collective-permute-done.9 = f32[4,2,2,512]{3,2,1,0:T(2,128)S(1)} collective-permute-done((f32[4,2,2,512]{3,2,1,0:T(2,128)S(1)}, f32[4,2,2,512]{3,2,1,0:T(2,128)S(1)}, u32[]{:S(2)}, u32[]{:S(2)}) %collective-permute-start.9) | collective-permute-done | bytes 32800 | tf_op jit(solution)/shard_map/ppermute | solution.py:345
  86.7 0.1 multiply_add_fusion
  86.8 0.7 reshape.52.refs_8_
  87.5 38.7 %local_grads.1 = (f32[4,2,128,512]{3,2,1,0:T(8,128)}, f32[4,2,128,512]{3,2,1,0:T(8,128)}, bf16[2048,256]{1,0:T(8,128)(2,1)}) custom-call(s32[32]{0:T(128)} %copy-done.11, s32[32]{0:T(128)} %select_reduce_fusion.place_ref, s32[16]{0:T(128)} %convert_reduce_fusion.2.n_ref, s32[16]{0:T(128)} %copy-done.7, bf16[2,1040,128]{2,1,0:T(8,128)(2,1)} %make_messages.1.refs_0_, ...), custom_call_target="tpu_custom_call" | custom-call | flops 21474836480 | bytes 8388608 | tf_op jit(solution)/shard_map/local_grads/pallas_call | solution.py:320
  126.1 0.3 collective-permute-start.11
  126.5 30.0 %all_to_all.17 = bf16[16,128,256]{2,1,0:T(8,128)(2,1)S(1)} all-to-all(bf16[16,128,256]{2,1,0:T(8,128)(2,1)} %bitcast.36), channel_id=1, replica_groups=mesh['x'=4,'zl'=2,'core'=2,'zh'=2,'y'=4] {'x','zl','zh'}, dimensions={0} | all-to-all | bytes 2097152 | tf_op jit(solution)/shard_map/all_to_all | solution.py:397
  156.5 0.1 convert_reduce_fusion
  156.7 0.0 collective-permute-done.11
  156.7 0.5 fusion.10
  157.2 0.1 slice_bitcast_fusion.1
  157.3 0.1 collective-permute-start.14
  157.3 0.1 collective-permute-start.13
  157.4 2.7 %collective-permute-start.12 = (bf16[2,128,512]{2,1,0:T(8,128)(2,1)S(1)}, bf16[2,128,512]{2,1,0:T(8,128)(2,1)S(1)}, u32[]{:S(2)}, u32[]{:S(2)}) collective-permute-start(bf16[2,128,512]{2,1,0:T(8,128)(2,1)S(1)} %get-tuple-element.13), channel_id=1, source_target_pairs={{0,3},{1,0},{2,1},{3,2},{4,7},{5,4},{6,5},{7,6},{8,11},{9,8},{10,9... | collective-permute-start | bytes 786440 | tf_op jit(solution)/shard_map/ppermute | solution.py:345
  160.1 0.7 fusion.11
  160.8 0.8 slice_bitcast_fusion.refs_0_
  161.6 3.7 %collective-permute-done.14.refs_3_ = bf16[2,128,512]{2,1,0:T(8,128)(2,1)S(1)} collective-permute-done((bf16[2,128,512]{2,1,0:T(8,128)(2,1)S(1)}, bf16[2,128,512]{2,1,0:T(8,128)(2,1)S(1)}, u32[]{:S(2)}, u32[]{:S(2)}) %collective-permute-start.14) | collective-permute-done | bytes 262176 | tf_op jit(solution)/shard_map/ppermute | solution.py:345
  165.3 7.0 %collective-permute-done.13.refs_2_ = bf16[2,128,512]{2,1,0:T(8,128)(2,1)S(1)} collective-permute-done((bf16[2,128,512]{2,1,0:T(8,128)(2,1)S(1)}, bf16[2,128,512]{2,1,0:T(8,128)(2,1)S(1)}, u32[]{:S(2)}, u32[]{:S(2)}) %collective-permute-start.13) | collective-permute-done | bytes 262176 | tf_op jit(solution)/shard_map/ppermute | solution.py:345
  172.3 0.0 collective-permute-done.12.refs_1_
  172.3 0.7 copy-done.4
  173.0 0.7 copy-done.5
  173.7 2.2 %finish_queries.1 = bf16[128,1024]{1,0:T(8,128)(2,1)} custom-call(f32[2,128,512]{2,1,0:T(8,128)} %slice_bitcast_fusion.refs_0_, bf16[2,128,512]{2,1,0:T(8,128)(2,1)} %copy-done.5, bf16[2,128,512]{2,1,0:T(8,128)(2,1)} %copy-done.4, bf16[2,128,512]{2,1,0:T(8,128)(2,1)} %copy-done.3), custom_call_target="tpu_custom_call" | custom-call | tf_op jit(solution)/shard_map/finish_queries/pallas_call | solution.py:97
  (25 shorter events, 0.2 us)
Async XLA Ops:
  2.8 14.1 %copy-start.2 = (bf16[2,1040,128]{2,1,0:T(8,128)(2,1)S(1)}, bf16[2,1040,128]{2,1,0:T(8,128)(2,1)}, u32[]{:S(2)}) copy-start(bf16[2,1040,128]{2,1,0:T(8,128)(2,1)} %make_messages.1.refs_0_) | copy-start | bytes 1597444
  2.8 16.0 %copy-start.6 = (s32[256]{0:T(256)S(1)}, s32[256]{0:T(256)}, u32[]{:S(2)}) copy-start(s32[256]{0:T(256)} %param.11) | copy-start | bytes 3076
  2.8 25.9 %collective-permute-start.5 = (bf16[2,1040,128]{2,1,0:T(8,128)(2,1)}, bf16[2,1040,128]{2,1,0:T(8,128)(2,1)S(1)}, u32[]{:S(2)}, u32[]{:S(2)}) collective-permute-start(bf16[2,1040,128]{2,1,0:T(8,128)(2,1)} %make_messages.1.refs_0_), channel_id=1, source_target_pairs={{0,3},{1,0},{2,1},{3,2},{4,7},{5,4},{6,5},{7,6},{8,11},{9,8},{10,9... | collective-permute-start | bytes 1597448 | tf_op jit(solution)/shard_map/ppermute | solution.py:345
  6.3 24.0 %collective-permute-start.3 = (bf16[2,1040,128]{2,1,0:T(8,128)(2,1)}, bf16[2,1040,128]{2,1,0:T(8,128)(2,1)S(1)}, u32[]{:S(2)}, u32[]{:S(2)}) collective-permute-start(bf16[2,1040,128]{2,1,0:T(8,128)(2,1)} %make_messages.1.refs_0_), channel_id=1, source_target_pairs={{0,2},{1,3},{2,0},{3,1},{4,6},{5,7},{6,4},{7,5},{8,10},{9,11},{10,... | collective-permute-start | bytes 1597448 | tf_op jit(solution)/shard_map/ppermute | solution.py:345
  6.7 26.8 %collective-permute-start.1 = (bf16[2,1040,128]{2,1,0:T(8,128)(2,1)}, bf16[2,1040,128]{2,1,0:T(8,128)(2,1)S(1)}, u32[]{:S(2)}, u32[]{:S(2)}) collective-permute-start(bf16[2,1040,128]{2,1,0:T(8,128)(2,1)} %make_messages.1.refs_0_), channel_id=1, source_target_pairs={{0,1},{1,2},{2,3},{3,0},{4,5},{5,6},{6,7},{7,4},{8,9},{9,10},{10,1... | collective-permute-start | bytes 1597448 | tf_op jit(solution)/shard_map/ppermute | solution.py:345
  9.2 26.3 %all-to-all-start = ((bf16[16,128,256]{2,1,0:T(8,128)(2,1)}), bf16[16,128,256]{2,1,0:T(8,128)(2,1)S(1)}, u32[]{:S(2)}, u32[]{:S(2)}) async-start(bf16[16,128,256]{2,1,0:T(8,128)(2,1)} %tile.2), calls=%async_computation | async-start | bytes 2097152 | tf_op jit(solution)/shard_map/all_to_all | solution.py:365
  16.9 18.7 %collective-permute-start = (bf16[2,1040,128]{2,1,0:T(8,128)(2,1)S(1)}, bf16[2,1040,128]{2,1,0:T(8,128)(2,1)}, u32[]{:S(2)}, u32[]{:S(2)}) collective-permute-start(bf16[2,1040,128]{2,1,0:T(8,128)(2,1)S(1)} %copy-done.2), channel_id=1, source_target_pairs={{0,8},{8,0},{1,9},{9,1},{2,10},{10,2},{3,11},{11,3},{4,12},{12,4},... | collective-permute-start | bytes 1597448 | tf_op jit(solution)/shard_map/ppermute | solution.py:345
  28.7 7.0 %copy-start.8 = (bf16[2,1040,128]{2,1,0:T(8,128)(2,1)}, bf16[2,1040,128]{2,1,0:T(8,128)(2,1)S(1)}, u32[]{:S(2)}) copy-start(bf16[2,1040,128]{2,1,0:T(8,128)(2,1)S(1)} %collective-permute-done.5.refs_6_) | copy-start | bytes 1597444
  28.7 6.8 %collective-permute-start.6 = (bf16[2,1040,128]{2,1,0:T(8,128)(2,1)S(1)}, bf16[2,1040,128]{2,1,0:T(8,128)(2,1)}, u32[]{:S(2)}, u32[]{:S(2)}) collective-permute-start(bf16[2,1040,128]{2,1,0:T(8,128)(2,1)S(1)} %collective-permute-done.5.refs_6_), channel_id=1, source_target_pairs={{0,8},{8,0},{1,9},{9,1},{2,10},{10,2},{3,11},{11,3},{4,12},{12,4},... | collective-permute-start | bytes 1597448 | tf_op jit(solution)/shard_map/ppermute | solution.py:345
  30.4 5.3 %copy-start.9 = (bf16[2,1040,128]{2,1,0:T(8,128)(2,1)}, bf16[2,1040,128]{2,1,0:T(8,128)(2,1)S(1)}, u32[]{:S(2)}) copy-start(bf16[2,1040,128]{2,1,0:T(8,128)(2,1)S(1)} %collective-permute-done.3.refs_4_) | copy-start | bytes 1597444
  30.4 5.1 %collective-permute-start.4 = (bf16[2,1040,128]{2,1,0:T(8,128)(2,1)S(1)}, bf16[2,1040,128]{2,1,0:T(8,128)(2,1)}, u32[]{:S(2)}, u32[]{:S(2)}) collective-permute-start(bf16[2,1040,128]{2,1,0:T(8,128)(2,1)S(1)} %collective-permute-done.3.refs_4_), channel_id=1, source_target_pairs={{0,8},{8,0},{1,9},{9,1},{2,10},{10,2},{3,11},{11,3},{4,12},{12,4},... | collective-permute-start | bytes 1597448 | tf_op jit(solution)/shard_map/ppermute | solution.py:345
  33.5 2.2 %copy-start.10 = (bf16[2,1040,128]{2,1,0:T(8,128)(2,1)}, bf16[2,1040,128]{2,1,0:T(8,128)(2,1)S(1)}, u32[]{:S(2)}) copy-start(bf16[2,1040,128]{2,1,0:T(8,128)(2,1)S(1)} %collective-permute-done.1.refs_2_) | copy-start | bytes 1597444
  33.5 2.2 %collective-permute-start.2 = (bf16[2,1040,128]{2,1,0:T(8,128)(2,1)S(1)}, bf16[2,1040,128]{2,1,0:T(8,128)(2,1)}, u32[]{:S(2)}, u32[]{:S(2)}) collective-permute-start(bf16[2,1040,128]{2,1,0:T(8,128)(2,1)S(1)} %collective-permute-done.1.refs_2_), channel_id=1, source_target_pairs={{0,8},{8,0},{1,9},{9,1},{2,10},{10,2},{3,11},{11,3},{4,12},{12,4},... | collective-permute-start | bytes 1597448 | tf_op jit(solution)/shard_map/ppermute | solution.py:345
  34.1 1.6 copy-start.7
  34.2 1.5 copy-start.11
  35.5 1.0 copy-start.1
  78.3 1.3 collective-permute-start.7
  79.7 4.0 %collective-permute-start.10 = (f32[4,2,2,512]{3,2,1,0:T(2,128)S(1)}, f32[4,2,2,512]{3,2,1,0:T(2,128)S(1)}, u32[]{:S(2)}, u32[]{:S(2)}) collective-permute-start(f32[4,2,2,512]{3,2,1,0:T(2,128)S(1)} %multiply_add_fusion.1), channel_id=1, source_target_pairs={{0,1},{1,2},{2,3},{3,0},{4,5},{5,6},{6,7},{7,4},{8,9},{9,10},{10,1... | collective-permute-start | bytes 98312 | tf_op jit(solution)/shard_map/ppermute | solution.py:345
  79.7 4.0 %collective-permute-start.8 = (f32[4,2,2,512]{3,2,1,0:T(2,128)S(1)}, f32[4,2,2,512]{3,2,1,0:T(2,128)S(1)}, u32[]{:S(2)}, u32[]{:S(2)}) collective-permute-start(f32[4,2,2,512]{3,2,1,0:T(2,128)S(1)} %multiply_add_fusion.1), channel_id=1, source_target_pairs={{0,3},{1,0},{2,1},{3,2},{4,7},{5,4},{6,5},{7,6},{8,11},{9,8},{10,9... | collective-permute-start | bytes 98312 | tf_op jit(solution)/shard_map/ppermute | solution.py:345
  82.4 4.3 %collective-permute-start.9 = (f32[4,2,2,512]{3,2,1,0:T(2,128)S(1)}, f32[4,2,2,512]{3,2,1,0:T(2,128)S(1)}, u32[]{:S(2)}, u32[]{:S(2)}) collective-permute-start(f32[4,2,2,512]{3,2,1,0:T(2,128)S(1)} %multiply_add_fusion.1), channel_id=1, source_target_pairs={{0,2},{1,3},{2,0},{3,1},{4,6},{5,7},{6,4},{7,5},{8,10},{9,11},{10,... | collective-permute-start | bytes 98312 | tf_op jit(solution)/shard_map/ppermute | solution.py:345
  126.1 30.5 %copy-start = (f32[4,2,128,512]{3,2,1,0:T(8,128)S(1)}, f32[4,2,128,512]{3,2,1,0:T(8,128)}, u32[]{:S(2)}) copy-start(f32[4,2,128,512]{3,2,1,0:T(8,128)} %get-tuple-element.6) | copy-start | bytes 6291460
  126.1 30.5 %collective-permute-start.11 = (f32[4,2,128,512]{3,2,1,0:T(8,128)}, f32[4,2,128,512]{3,2,1,0:T(8,128)S(1)}, u32[]{:S(2)}, u32[]{:S(2)}) collective-permute-start(f32[4,2,128,512]{3,2,1,0:T(8,128)} %get-tuple-element.7), channel_id=1, source_target_pairs={{0,8},{8,0},{1,9},{9,1},{2,10},{10,2},{3,11},{11,3},{4,12},{12,4},... | collective-permute-start | bytes 6291464 | tf_op jit(solution)/shard_map/ppermute | solution.py:345
  157.3 8.0 %collective-permute-start.14 = (bf16[2,128,512]{2,1,0:T(8,128)(2,1)S(1)}, bf16[2,128,512]{2,1,0:T(8,128)(2,1)S(1)}, u32[]{:S(2)}, u32[]{:S(2)}) collective-permute-start(bf16[2,128,512]{2,1,0:T(8,128)(2,1)S(1)} %get-tuple-element.11), channel_id=1, source_target_pairs={{0,2},{1,3},{2,0},{3,1},{4,6},{5,7},{6,4},{7,5},{8,10},{9,11},{10,... | collective-permute-start | bytes 786440 | tf_op jit(solution)/shard_map/ppermute | solution.py:345
  157.3 14.9 %collective-permute-start.13 = (bf16[2,128,512]{2,1,0:T(8,128)(2,1)S(1)}, bf16[2,128,512]{2,1,0:T(8,128)(2,1)S(1)}, u32[]{:S(2)}, u32[]{:S(2)}) collective-permute-start(bf16[2,128,512]{2,1,0:T(8,128)(2,1)S(1)} %get-tuple-element.12), channel_id=1, source_target_pairs={{0,1},{1,2},{2,3},{3,0},{4,5},{5,6},{6,7},{7,4},{8,9},{9,10},{10,1... | collective-permute-start | bytes 786440 | tf_op jit(solution)/shard_map/ppermute | solution.py:345
  157.4 14.8 %collective-permute-start.12 = (bf16[2,128,512]{2,1,0:T(8,128)(2,1)S(1)}, bf16[2,128,512]{2,1,0:T(8,128)(2,1)S(1)}, u32[]{:S(2)}, u32[]{:S(2)}) collective-permute-start(bf16[2,128,512]{2,1,0:T(8,128)(2,1)S(1)} %get-tuple-element.13), channel_id=1, source_target_pairs={{0,3},{1,0},{2,1},{3,2},{4,7},{5,4},{6,5},{7,6},{8,11},{9,8},{10,9... | collective-permute-start | bytes 786440 | tf_op jit(solution)/shard_map/ppermute | solution.py:345
  165.3 7.0 %copy-start.3 = (bf16[2,128,512]{2,1,0:T(8,128)(2,1)}, bf16[2,128,512]{2,1,0:T(8,128)(2,1)S(1)}, u32[]{:S(2)}) copy-start(bf16[2,128,512]{2,1,0:T(8,128)(2,1)S(1)} %collective-permute-done.14.refs_3_) | copy-start | bytes 786436
  172.3 0.7 copy-start.4
  173.0 0.7 copy-start.5

commit v3 on v2

v3 whole, which is shorter than its diff:
```python
import functools
import math

import jax
import jax.numpy as jnp
from jax import lax
from jax.experimental import pallas as pl
from jax.experimental.pallas import tpu as pltpu
from jax.sharding import Mesh, PartitionSpec as P

DH = 128
HEADS = 8
BLOCK = 64
ROWS = HEADS * BLOCK
GRAD_ROWS = ROWS + 16
SCALE = DH ** -0.5
C2 = SCALE * math.log2(math.e)
NEG = -1e30
KB = 4
KT = KB * BLOCK
UNROLL = 8
VMEM_LIMIT = 56 * 1024 * 1024
F32 = jnp.float32
BF16 = jnp.bfloat16
KEY_AXES = ("x", "zl", "zh")
SMEM = pl.BlockSpec(memory_space=pltpu.SMEM)
VMEM = pl.BlockSpec(memory_space=pltpu.VMEM)


def nn(a, b):
    return lax.dot_general(a, b, (((1,), (0,)), ((), ())), preferred_element_type=F32)


def nt(a, b):
    return lax.dot_general(a, b, (((1,), (1,)), ((), ())), preferred_element_type=F32)


def params():
    return pltpu.CompilerParams(vmem_limit_bytes=VMEM_LIMIT)


def cost(products, nq, count):
    area = nq * ROWS * count // 2
    return pl.CostEstimate(flops=products * 4 * area * DH, bytes_accessed=8 << 20, transcendentals=area)


def message_kernel(q_ref, g_ref, o_ref, query_ref, grad_ref):
    for blk in range(2):
        tokens = slice(blk * BLOCK, (blk + 1) * BLOCK)
        parts = []
        for h in range(HEADS):
            lanes = slice(h * DH, (h + 1) * DH)
            g = g_ref[tokens, lanes]
            query_ref[blk, h * BLOCK:(h + 1) * BLOCK, :] = q_ref[tokens, lanes]
            grad_ref[blk, h * BLOCK:(h + 1) * BLOCK, :] = g
            parts.append(g.astype(F32) * o_ref[tokens, lanes].astype(F32))
        delta = jnp.sum(jnp.concatenate(parts, 0).T, axis=0, keepdims=True)
        rows = []
        rest = delta
        for _ in range(3):
            part = rest.astype(BF16).astype(F32)
            rest = rest - part
            rows += [part[:, c * DH:(c + 1) * DH] for c in range(ROWS // DH)]
        rows.append(jnp.zeros((16 - len(rows), DH), F32))
        grad_ref[blk, ROWS:, :] = jnp.concatenate(rows, 0).astype(BF16)


def make_messages(queries, out_grad, outputs):
    return pl.pallas_call(
        message_kernel,
        out_shape=(
            jax.ShapeDtypeStruct((2, ROWS, DH), BF16),
            jax.ShapeDtypeStruct((2, GRAD_ROWS, DH), BF16),
        ),
        in_specs=[VMEM] * 3,
        out_specs=(VMEM,) * 2,
        compiler_params=params(),
        name="make_messages",
    )(queries, out_grad, outputs)


def finish_kernel(*refs):
    out_ref = refs[-1]
    for blk in range(2):
        total = refs[0][blk]
        for other in refs[1:4]:
            total = total + other[blk].astype(F32)
        total = total.T.astype(BF16)
        for h in range(HEADS):
            out_ref[blk * BLOCK:(blk + 1) * BLOCK, h * DH:(h + 1) * DH] = total[h * BLOCK:(h + 1) * BLOCK]


def finish_queries(parts):
    return pl.pallas_call(
        finish_kernel,
        out_shape=jax.ShapeDtypeStruct((2 * BLOCK, HEADS * DH), BF16),
        in_specs=[VMEM] * 4,
        out_specs=VMEM,
        compiler_params=params(),
        name="finish_queries",
    )(*parts)


def sort_blocks(table, src, lanes, dst, start, nk):
    def body(j, c):
        r = pl.multiple_of(table.rank(start + j) * BLOCK, BLOCK)
        dst[pl.ds(r, BLOCK), :] = src[pl.ds(pl.multiple_of(j * BLOCK, BLOCK), BLOCK), lanes]
        return c

    lax.fori_loop(0, nk, body, 0, unroll=4)


class Table:
    def __init__(self, ref, nq, nk):
        size = list_size(nq, nk)
        starts = [0]
        for n in (nk, nk, nq, nq, size, size, size, 1):
            starts.append(starts[-1] + n)
        self.ref, self.starts = ref, starts

    def rank(self, j):
        return self.ref[self.starts[0] + j]

    def place(self, j):
        return self.ref[self.starts[1] + j]

    def visible(self, b):
        return self.ref[self.starts[2] + b]

    def query_place(self, b):
        return self.ref[self.starts[3] + b]

    def entry(self, w):
        return tuple(self.ref[self.starts[i] + w] for i in (4, 5, 6))

    def end(self):
        return self.ref[self.starts[7]]


def list_size(nq, nk):
    return nq * ((nk + KB - 1) // KB) + UNROLL + 2


def make_table(rank, place, query_place, key_place):
    nq, nk = query_place.shape[0], key_place.shape[0]
    visible = jnp.sum(key_place[None, :] <= query_place[:, None], axis=1, dtype=jnp.int32)
    count = (visible + KB - 1) // KB
    earlier = jnp.arange(nq)[:, None] > jnp.arange(nq)[None, :]
    start = jnp.sum(jnp.where(earlier, count[None, :], 0), axis=1, dtype=jnp.int32) + 1
    w = jnp.arange(list_size(nq, nk), dtype=jnp.int32)[:, None]
    inside = (w >= start[None, :]) & (w < (start + count)[None, :])

    def pick(a):
        return jnp.sum(jnp.where(inside, a, 0), axis=1, dtype=jnp.int32)

    ids = jnp.arange(nq, dtype=jnp.int32)[None, :]
    lists = [pick(ids), pick(w - start[None, :]), pick(query_place[None, :] + 1) - 1]
    end = jnp.sum(count, dtype=jnp.int32).reshape(1) + 1
    return jnp.concatenate([rank, place, visible, query_place, *lists, end])


def run_work(end, prepare, use):
    def steps(unroll, first):
        def body(i, c):
            for u in range(unroll):
                w = first + i * unroll + u
                prepare(w + 1, (u + 1) % 2)
                use(w, u % 2)
            return c

        return body

    long = end // UNROLL
    lax.fori_loop(0, long, steps(UNROLL, 0), 0)
    rest = long * UNROLL
    lax.fori_loop(0, (end - rest + 1) // 2, steps(2, rest), 0)


def difference():
    key = lax.broadcasted_iota(jnp.int32, (BLOCK, ROWS), 0)
    query = lax.broadcasted_iota(jnp.int32, (BLOCK, ROWS), 1) % BLOCK
    return key - query


def causal(s, table, t, query_place, diff):
    parts = []
    for u in range(KB):
        place = table.place(t * KB + u)
        limit = jnp.where(place < query_place, BLOCK, jnp.where(place == query_place, 0, -2 * BLOCK))
        parts.append(jnp.where(diff <= limit, s[u * BLOCK:(u + 1) * BLOCK], NEG))
    return jnp.concatenate(parts, 0)


def combine(parts):
    top = functools.reduce(jnp.maximum, parts)
    return top + jnp.log2(sum(jnp.exp2(part - top) for part in parts))


def lse_kernel(nq, nk, table_ref, *refs):
    table = Table(table_ref, nq, nk)
    pieces, columns, refs = refs[:4], refs[4:6], refs[6:]
    lse_ref, ks, vs, kst, q_all, s_buf, diff, l8, m8 = refs
    for i, column in enumerate(columns):
        sort_blocks(table, column, slice(0, DH), ks, i * nk // 2, nk // 2)
        sort_blocks(table, column, slice(DH, 2 * DH), vs, i * nk // 2, nk // 2)
    kst[...] = ks[...].T
    for i, piece in enumerate(pieces):
        q_all[2 * i:2 * i + 2] = piece[...]
    diff[...] = difference()
    l8[...] = jnp.zeros_like(l8)

    def prepare(w, slot):
        b, t, _ = table.entry(w)
        keys = ks[pl.ds(pl.multiple_of(t * KT, KT), KT), :]
        s_buf[slot] = nt(keys, q_all[b])

    def use(w, slot):
        b, t, qp = table.entry(w)
        s = causal(s_buf[slot] * C2, table, t, qp, diff[...])
        l8[b] += jnp.sum(jnp.exp2(s).reshape(KT // 8, 8, ROWS), axis=0)

    run_work(table.end(), prepare, use)
    fine = jnp.ones((1, ROWS), F32)
    for b in range(nq):
        total = jnp.sum(l8[b], axis=0, keepdims=True)
        seen = table.visible(b) > 0
        inside = jnp.where((total > 1e-18) & (total < 1e30), 1.0, 0.0)
        fine = jnp.minimum(fine, jnp.where(seen, inside, 1.0))
        lse_ref[b:b + 1, :] = jnp.where(seen, jnp.log2(total), NEG)

    @pl.when(jnp.min(fine) < 0.5)
    def _():
        def block(b, c):
            m8[...] = jnp.full_like(m8, 0.5 * NEG)
            l8[0] = jnp.zeros((8, ROWS), F32)

            def tile(t, c):
                keys = ks[pl.ds(pl.multiple_of(t * KT, KT), KT), :]
                s = causal(nt(keys, q_all[b]) * C2, table, t, table.query_place(b), diff[...])
                s = s.reshape(KT // 8, 8, ROWS)
                m = m8[...]
                top = jnp.maximum(m, jnp.max(s, axis=0))
                l8[0] = l8[0] * jnp.exp2(m - top) + jnp.sum(jnp.exp2(s - top[None]), axis=0)
                m8[...] = top
                return c

            lax.fori_loop(0, (table.visible(b) + KB - 1) // KB, tile, 0)
            m = m8[...]
            top = jnp.max(m, axis=0, keepdims=True)
            total = jnp.sum(l8[0] * jnp.exp2(m - top), axis=0, keepdims=True)
            lse_ref[pl.ds(b, 1), :] = jnp.where(table.visible(b) > 0, top + jnp.log2(total), NEG)
            return c

        lax.fori_loop(0, nq, block, 0)


def local_lse(table, pieces, columns):
    nq = 8
    count = 2 * columns[0].shape[0]
    nk = count // BLOCK
    row_shape = jax.ShapeDtypeStruct((count, DH), BF16)
    return pl.pallas_call(
        functools.partial(lse_kernel, nq, nk),
        out_shape=(
            jax.ShapeDtypeStruct((nq, ROWS), F32),
            row_shape,
            row_shape,
            jax.ShapeDtypeStruct((DH, count), BF16),
        ),
        in_specs=[SMEM] + [VMEM] * 6,
        out_specs=(VMEM,) * 4,
        scratch_shapes=[
            pltpu.VMEM((nq, ROWS, DH), BF16),
            pltpu.VMEM((2, KT, ROWS), F32),
            pltpu.VMEM((BLOCK, ROWS), jnp.int32),
            pltpu.VMEM((nq, 8, ROWS), F32),
            pltpu.VMEM((8, ROWS), F32),
        ],
        compiler_params=params(),
        cost_estimate=cost(1, nq, count),
        name="local_lse",
    )(table, *pieces, *columns)


def grad_kernel(nq, nk, table_ref, *refs):
    table = Table(table_ref, nq, nk)
    queries, grads, refs = refs[:4], refs[4:8], refs[8:]
    sums_in, (ks, vs, kst), refs = refs[:4], refs[4:7], refs[7:]
    query_out, kv_out, kv_send, refs = refs[:4], refs[4], refs[5], refs[6:]
    q_all, g_all, lse, delta, sums, dqa, s_buf, dp_buf, diff = refs
    for i in range(4):
        for j in range(2):
            b = 2 * i + j
            lse[b] = combine([sums_in[d][b2:b2 + 1, :] for d in range(4) for b2 in [2 * ((i + d) % 4) + j]])
            q_all[b] = queries[i][j]
            g_all[b] = grads[i][j, :ROWS, :]
            tail = grads[i][j, ROWS:, :].astype(F32)
            n = ROWS // DH
            tail = tail[0:n] + tail[n:2 * n] + tail[2 * n:3 * n]
            for c in range(n):
                delta[b, :, c * DH:(c + 1) * DH] = tail[c:c + 1]
    sums[...] = jnp.zeros_like(sums)
    dqa[...] = jnp.zeros_like(dqa)
    s_buf[0] = jnp.zeros((KT, ROWS), F32)
    dp_buf[0] = jnp.zeros((KT, ROWS), F32)
    diff[...] = difference()

    def prepare(w, slot):
        b, t, _ = table.entry(w)
        at = pl.ds(pl.multiple_of(t * KT, KT), KT)
        s_buf[slot] = nt(ks[at, :], q_all[b])
        dp_buf[slot] = nt(vs[at, :], g_all[b])

    def use(w, slot):
        b, t, qp = table.entry(w)
        at = pl.ds(pl.multiple_of(t * KT, KT), KT)
        p = jnp.exp2(causal(s_buf[slot] * C2 - lse[b], table, t, qp, diff[...]))
        ds = (p * (dp_buf[slot] - delta[b])).astype(BF16)
        sums[1, at, :] += nn(p.astype(BF16), g_all[b])
        sums[0, at, :] += nn(ds, q_all[b])
        dqa[b] += nn(kst[:, at], ds)

    run_work(table.end(), prepare, use)
    for i in range(4):
        for j in range(2):
            query_out[i][j] = (dqa[2 * i + j] * SCALE).astype(query_out[i].dtype)

    for i, out in enumerate((kv_out, kv_send)):
        def body(j, c):
            r = pl.ds(pl.multiple_of(table.rank(i * nk // 2 + j) * BLOCK, BLOCK), BLOCK)
            at = pl.ds(pl.multiple_of(j * BLOCK, BLOCK), BLOCK)
            out[at, :DH] = (sums[0, r, :] * SCALE).astype(out.dtype)
            out[at, DH:] = sums[1, r, :].astype(out.dtype)
            return c

        lax.fori_loop(0, nk // 2, body, 0, unroll=2)


def local_grads(table, queries, grads, sums, sorted_keys):
    nq = 8
    count = sorted_keys[0].shape[0]
    nk = count // BLOCK
    return pl.pallas_call(
        functools.partial(grad_kernel, nq, nk),
        out_shape=tuple(jax.ShapeDtypeStruct((2, DH, ROWS), F32 if i == 0 else BF16) for i in range(4))
        + tuple(jax.ShapeDtypeStruct((count // 2, 2 * DH), t) for t in (F32, BF16)),
        in_specs=[SMEM] + [VMEM] * 15,
        out_specs=(VMEM,) * 6,
        scratch_shapes=[
            pltpu.VMEM((nq, ROWS, DH), BF16),
            pltpu.VMEM((nq, ROWS, DH), BF16),
            pltpu.VMEM((nq, 1, ROWS), F32),
            pltpu.VMEM((nq, 1, ROWS), F32),
            pltpu.VMEM((2, count, DH), F32),
            pltpu.VMEM((nq, DH, ROWS), F32),
            pltpu.VMEM((2, KT, ROWS), F32),
            pltpu.VMEM((2, KT, ROWS), F32),
            pltpu.VMEM((BLOCK, ROWS), jnp.int32),
        ],
        compiler_params=params(),
        cost_estimate=cost(5, nq, count),
        name="local_grads",
    )(table, *queries, *grads, *sums, *sorted_keys)


def along(axis, shift, size, array):
    return lax.ppermute(array, axis, [(i, (i + shift) % size) for i in range(size)])


def gather_y(own):
    one, three, two = (along("y", s, 4, own) for s in (1, 3, 2))
    return [own, one, two, three]


def shards(queries, keys, values, outputs, out_grad, block_order):
    x, zl, core, zh, y = (lax.axis_index(a) for a in ("x", "zl", "core", "zh", "y"))
    fence = lax.optimization_barrier

    pair = jnp.concatenate([keys, values], axis=1)
    column = lax.all_to_all(jnp.tile(pair, (16, 1)), KEY_AXES, 0, 0, tiled=True)
    columns = [column, along("core", 1, 2, column)]

    order = block_order.reshape(4, 2, 2, 2, 4, 2)
    key_place = lax.dynamic_slice(order, (0, 0, 0, 0, y, 0), (4, 2, 2, 2, 1, 2))
    key_place = jnp.moveaxis(key_place, 2, 0).reshape(2, 32)
    key_place = jnp.where(core == 0, key_place, key_place[::-1]).reshape(64)
    here = lax.dynamic_slice(order, (x, zl, core, zh, 0, 0), (1, 1, 1, 1, 4, 2)).reshape(4, 2)
    query_place = jnp.stack([here[(y - s) % 4] for s in range(4)]).reshape(8)
    rank = jnp.sum(key_place[:, None] < key_place[None, :], axis=0, dtype=jnp.int32)
    spots = lax.broadcasted_iota(jnp.int32, (64, 64), 0)
    place = jnp.sum(jnp.where(rank[None, :] == spots, key_place[None, :], 0), axis=1, dtype=jnp.int32)
    table = make_table(rank, place, query_place, key_place)

    query_message, grad_message = make_messages(queries, out_grad, outputs)
    query_pieces = gather_y(query_message)
    grad_pieces = gather_y(grad_message)

    (part, *sorted_keys), grad_pieces[1:] = fence((local_lse(table, query_pieces, columns), grad_pieces[1:]))
    sums = [part] + [along("y", -d, 4, part) for d in (1, 2, 3)]

    *query_parts, kv_part, kv_send = local_grads(table, query_pieces, grad_pieces, sums, sorted_keys)
    query_parts = [query_parts[0]] + [along("y", -s, 4, query_parts[s]) for s in (1, 3, 2)]
    kv_part = (kv_part + along("core", 1, 2, kv_send).astype(F32)).astype(BF16)
    terms = lax.all_to_all(kv_part, KEY_AXES, 0, 0, tiled=True)
    kv_grad = jnp.sum(terms.astype(F32).reshape(16, 2 * BLOCK, 2 * DH), axis=0)
    return finish_queries(query_parts), kv_grad[:, :DH], kv_grad[:, DH:]


def solution(mesh):
    fine = Mesh(mesh.devices.reshape(4, 2, 2, 2, 4), ("x", "zl", "core", "zh", "y"))
    rows = P(("x", "zl", "core", "zh", "y"), None)
    return jax.shard_map(
        shards,
        mesh=fine,
        in_specs=(rows,) * 5 + (P(),),
        out_specs=(rows,) * 3,
        check_vma=False,
    )
```

time: 178 us -> 170 us (0.955); the launches traced: 176 us -> 170 us
  starting transfers between devices: 22.3 us -> 67.9 us
  blocking collectives: 30 us -> 0 us
  Pallas kernels: 83.9 us -> 66.7 us
  waiting for transfers between devices: 28.8 us -> 23.2 us
    all_to_all x1 -> x0, blocking collectives: 30 us -> none  [shards(): terms = lax.all_to_all(kv_part, KEY_AXES, 0, 0, tiled=True)]
    all_to_all x1 -> x2, starting transfers between devices: 7.6 us -> 33 us  [the longest x1 24.6 us: shards(): terms = lax.all_to_all(kv_part, KEY_AXES, 0, 0, tiled=True)]
    ppermute x15 -> x14, starting transfers between devices: 14.7 us -> 34.9 us  [along(): lax.ppermute(array, axis, [(i, (i + shift) % size) for i in range(size)])]
    pallas_call x3, Pallas kernels: 81.7 us -> 64.5 us  [the longest x1 33.2 us: local_lse(): pl.pallas_call(functools.partial(lse_kernel, nq, nk), out_shape=(jax.Shap...]
    ppermute x15 -> x14, waiting for transfers between devices: 28.8 us -> 15.2 us  [along(): lax.ppermute(array, axis, [(i, (i + shift) % size) for i in range(size)])]
    all_to_all x1 -> x2, waiting for transfers between devices: 0.01 us -> 7.95 us  [the longest x1 7.95 us: shards(): column = lax.all_to_all(jnp.tile(pair, (16, 1)), KEY_AXES, 0, 0, tiled=True)]
    convert_element_type x0 -> x1, other arithmetic: none -> 2.88 us  [shards(): kv_part = (kv_part + along('core', 1, 2, kv_send).astype(F32)).astype(BF16)]
  transfers between devices with their start and end apart: 16 -> 16, of which waited for: 8 -> 5; matrix products, arithmetic and copies ran while one was open for 3% -> 1% of each run, Pallas kernels for 0% -> 22%
where the time goes in v3:
time: 170 us
  starting transfers between devices  67.9 us (40%)
  Pallas kernels  66.7 us (39%)
  waiting for transfers between devices  23.2 us (14%)
  local copies, waits for them, and re-layouts  6.01 us (4%)
  other arithmetic  5.06 us (3%)
    ppermute x14, starting transfers between devices, along(): lax.ppermute(array, axis, [(i, (i + shift) % size) for i in range(size)])  34.9 us
    pallas_call x1, Pallas kernels, local_lse(): pl.pallas_call(functools.partial(lse_kernel, nq, nk), out_shape=(jax.Shap...  33.2 us
    pallas_call x1, Pallas kernels, local_grads(): pl.pallas_call(functools.partial(grad_kernel, nq, nk), out_shape=tuple((j...  29.2 us
    all_to_all x1, starting transfers between devices, shards(): terms = lax.all_to_all(kv_part, KEY_AXES, 0, 0, tiled=True)  24.6 us
    ppermute x14, waiting for transfers between devices, along(): lax.ppermute(array, axis, [(i, (i + shift) % size) for i in range(size)])  15.2 us
    all_to_all x1, starting transfers between devices, shards(): column = lax.all_to_all(jnp.tile(pair, (16, 1)), KEY_AXES, 0, 0, tiled=True)  8.43 us
    all_to_all x1, waiting for transfers between devices, shards(): column = lax.all_to_all(jnp.tile(pair, (16, 1)), KEY_AXES, 0, 0, tiled=True)  7.95 us
  transfers between devices with their start and end apart: 16, of which 5 were waited for; matrix products, arithmetic and copies ran while one was open for 1% of the time, Pallas kernels for 22%

profile of v3, /device:TPU:1, one launch (start us, length us, event | category | flops | bytes accessed | tf_op | source)
XLA Modules:
  0.0 170.3 jit_solution(1493887773952793991)
XLA Ops:
  0.6 0.8 pad_maximum_fusion
  1.4 1.1 tile.2
  2.5 8.4 %all-to-all-start = ((bf16[16,128,256]{2,1,0:T(8,128)(2,1)}), bf16[16,128,256]{2,1,0:T(8,128)(2,1)S(1)}, u32[]{:S(2)}, u32[]{:S(2)}) async-start(bf16[16,128,256]{2,1,0:T(8,128)(2,1)} %tile.2), calls=%async_computation | async-start | bytes 2097152 | tf_op jit(solution)/shard_map/all_to_all | solution.py:380
  10.9 2.1 %make_messages.1 = (bf16[2,512,128]{2,1,0:T(8,128)(2,1)}, bf16[2,528,128]{2,1,0:T(8,128)(2,1)}) custom-call(bf16[128,1024]{1,0:T(8,128)(2,1)} %q_ref.1, bf16[128,1024]{1,0:T(8,128)(2,1)} %g_ref.1, bf16[128,1024]{1,0:T(8,128)(2,1)} %o_ref.1), custom_call_target="tpu_custom_call" | custom-call | tf_op jit(solution)/shard_map/make_messages/pallas_call | solution.py:69
  13.1 2.7 %collective-permute-start.2 = (bf16[2,512,128]{2,1,0:T(8,128)(2,1)}, bf16[2,512,128]{2,1,0:T(8,128)(2,1)S(1)}, u32[]{:S(2)}, u32[]{:S(2)}) collective-permute-start(bf16[2,512,128]{2,1,0:T(8,128)(2,1)} %get-tuple-element.22.refs_0_), channel_id=1, source_target_pairs={{0,3},{1,0},{2,1},{3,2},{4,7},{5,4},{6,5},{7,6},{8,11},{9,8},{10,9... | collective-permute-start | bytes 786440 | tf_op jit(solution)/shard_map/ppermute | solution.py:367
  15.8 0.3 collective-permute-start.1
  16.1 0.7 collective-permute-start
  16.8 2.0 %collective-permute-start.6 = (bf16[2,528,128]{2,1,0:T(8,128)(2,1)}, bf16[2,528,128]{2,1,0:T(8,128)(2,1)S(1)}, u32[]{:S(2)}, u32[]{:S(2)}) collective-permute-start(bf16[2,528,128]{2,1,0:T(8,128)(2,1)} %get-tuple-element.23.refs_4_), channel_id=1, source_target_pairs={{0,3},{1,0},{2,1},{3,2},{4,7},{5,4},{6,5},{7,6},{8,11},{9,8},{10,9... | collective-permute-start | bytes 811016 | tf_op jit(solution)/shard_map/ppermute | solution.py:367
  18.8 0.0 copy-done.4
  18.8 0.2 reshape.68
  19.0 0.1 reshape.69
  19.2 0.1 le.16
  19.3 0.1 lt.72
  19.4 0.2 convert_reduce_fusion.2
  19.6 8.0 %all-to-all-done = bf16[16,128,256]{2,1,0:T(8,128)(2,1)S(1)} async-done(((bf16[16,128,256]{2,1,0:T(8,128)(2,1)}), bf16[16,128,256]{2,1,0:T(8,128)(2,1)S(1)}, u32[]{:S(2)}, u32[]{:S(2)}) %all-to-all-start) | async-done | bytes 1048608 | tf_op jit(solution)/shard_map/all_to_all | solution.py:380
  27.5 2.6 %collective-permute-start.3 = (bf16[2048,256]{1,0:T(8,128)(2,1)S(1)}, bf16[2048,256]{1,0:T(8,128)(2,1)S(1)}, u32[]{:S(2)}, u32[]{:S(2)}) collective-permute-start(bf16[2048,256]{1,0:T(8,128)(2,1)S(1)} %bitcast.15), channel_id=1, source_target_pairs={{0,8},{8,0},{1,9},{9,1},{2,10},{10,2},{3,11},{11,3},{4,12},{12,4},... | collective-permute-start | bytes 3145736 | tf_op jit(solution)/shard_map/ppermute | solution.py:367
  30.1 0.6 fusion.6
  30.7 0.1 select_reduce_fusion.4
  30.8 0.1 convert_reduce_fusion.1
  30.9 0.1 select_reduce_fusion.1
  31.0 0.1 select_reduce_fusion
  31.8 0.7 concatenate.6.table_ref
  32.5 0.0 collective-permute-done.2.refs_3_
  32.5 2.9 %collective-permute-start.5 = (bf16[2,528,128]{2,1,0:T(8,128)(2,1)}, bf16[2,528,128]{2,1,0:T(8,128)(2,1)S(1)}, u32[]{:S(2)}, u32[]{:S(2)}) collective-permute-start(bf16[2,528,128]{2,1,0:T(8,128)(2,1)} %get-tuple-element.23.refs_4_), channel_id=1, source_target_pairs={{0,2},{1,3},{2,0},{3,1},{4,6},{5,7},{6,4},{7,5},{8,10},{9,11},{10,... | collective-permute-start | bytes 811016 | tf_op jit(solution)/shard_map/ppermute | solution.py:367
  35.4 0.0 collective-permute-done.1.refs_2_
  35.4 0.4 collective-permute-start.4
  35.8 0.0 collective-permute-done.refs_1_
  35.8 0.0 collective-permute-done.3.refs_5_
  35.8 0.0 copy-done
  35.8 0.0 copy-done.9
  35.8 0.3 copy-done.10
  36.1 0.4 copy-done.11
  36.6 1.0 copy-done.5
  37.6 33.2 %local_lse.1 = (f32[8,512]{1,0:T(8,128)}, bf16[4096,128]{1,0:T(8,128)(2,1)}, bf16[4096,128]{1,0:T(8,128)(2,1)}, bf16[128,4096]{1,0:T(8,128)(2,1)}) custom-call(s32[559]{0:T(1024)} %concatenate.6.table_ref, bf16[2,512,128]{2,1,0:T(8,128)(2,1)} %get-tuple-element.22.refs_0_, bf16[2,512,128]{2,1,0:T(8,128)(2,1)} %copy-done.11, bf16[2,512,128]{2,1,0:T(8,128)(2,1)} %copy-done.10, ...), custom_call_target="tpu_custom_call" | custom-call | flops 4294967296 | bytes 8388608 | tf_op jit(solution)/shard_map/local_lse/pallas_call | solution.py:262
  70.8 0.0 collective-permute-done.6.refs_7_
  70.8 0.0 collective-permute-done.5.refs_6_
  70.8 0.0 copy-start.7
  70.8 0.0 collective-permute-done.4.refs_5_
  70.8 3.7 %collective-permute-start.9 = (f32[8,512]{1,0:T(8,128)}, f32[8,512]{1,0:T(8,128)S(1)}, u32[]{:S(2)}, u32[]{:S(2)}) collective-permute-start(f32[8,512]{1,0:T(8,128)} %get-tuple-element.31.refs_8_), channel_id=1, source_target_pairs={{0,1},{1,2},{2,3},{3,0},{4,5},{5,6},{6,7},{7,4},{8,9},{9,10},{10,1... | collective-permute-start | bytes 49160 | tf_op jit(solution)/shard_map/ppermute | solution.py:367
  74.5 7.7 %collective-permute-start.8 = (f32[8,512]{1,0:T(8,128)}, f32[8,512]{1,0:T(8,128)S(1)}, u32[]{:S(2)}, u32[]{:S(2)}) collective-permute-start(f32[8,512]{1,0:T(8,128)} %get-tuple-element.31.refs_8_), channel_id=1, source_target_pairs={{0,2},{1,3},{2,0},{3,1},{4,6},{5,7},{6,4},{7,5},{8,10},{9,11},{10,... | collective-permute-start | bytes 49160 | tf_op jit(solution)/shard_map/ppermute | solution.py:367
  82.2 2.0 %collective-permute-start.7 = (f32[8,512]{1,0:T(8,128)}, f32[8,512]{1,0:T(8,128)S(1)}, u32[]{:S(2)}, u32[]{:S(2)}) collective-permute-start(f32[8,512]{1,0:T(8,128)} %get-tuple-element.31.refs_8_), channel_id=1, source_target_pairs={{0,3},{1,0},{2,1},{3,2},{4,7},{5,4},{6,5},{7,6},{8,11},{9,8},{10,9... | collective-permute-start | bytes 49160 | tf_op jit(solution)/shard_map/ppermute | solution.py:367
  84.2 0.0 collective-permute-done.9.refs_11_
  84.2 0.0 collective-permute-done.8.refs_10_
  84.2 1.1 collective-permute-done.7.refs_9_
  85.3 0.0 copy-done.7
  85.3 0.0 copy-start.17
  85.3 0.6 copy-done.17
  85.9 29.2 %local_grads.1 = (f32[2,128,512]{2,1,0:T(8,128)}, bf16[2,128,512]{2,1,0:T(8,128)(2,1)}, bf16[2,128,512]{2,1,0:T(8,128)(2,1)}, bf16[2,128,512]{2,1,0:T(8,128)(2,1...) custom-call(s32[559]{0:T(1024)} %concatenate.6.table_ref, bf16[2,512,128]{2,1,0:T(8,128)(2,1)} %get-tuple-element.22.refs_0_, ...), custom_call_target="tpu_custom_call" | custom-call | flops 21474836480 | bytes 8388608 | tf_op jit(solution)/shard_map/local_grads/pallas_call | solution.py:343
  115.1 0.0 collective-permute-start.13
  115.1 2.9 %collective-permute-done.13 = bf16[2048,256]{1,0:T(8,128)(2,1)S(1)} collective-permute-done((bf16[2048,256]{1,0:T(8,128)(2,1)}, bf16[2048,256]{1,0:T(8,128)(2,1)S(1)}, u32[]{:S(2)}, u32[]{:S(2)}) %collective-permute-start.13) | collective-permute-done | bytes 1048608 | tf_op jit(solution)/shard_map/ppermute | solution.py:367
  118.0 2.9 %add_convert_fusion = bf16[2048,256]{1,0:T(8,128)(2,1)} fusion(f32[2048,256]{1,0:T(8,128)} %get-tuple-element.39, bf16[2048,256]{1,0:T(8,128)(2,1)S(1)} %collective-permute-done.13), kind=kLoop, calls=%fused_computation.1 | loop fusion | flops 1572864 | bytes 4194304 | tf_op jit(solution)/shard_map/convert_element_type | solution.py:403
  120.9 24.6 %all-to-all-start.1 = ((bf16[16,128,256]{2,1,0:T(8,128)(2,1)}), bf16[16,128,256]{2,1,0:T(8,128)(2,1)S(1)}, u32[]{:S(2)}, u32[]{:S(2)}) async-start(bf16[16,128,256]{2,1,0:T(8,128)(2,1)} %bitcast.7), calls=%async_computation.1 | async-start | bytes 2097152 | tf_op jit(solution)/shard_map/all_to_all | solution.py:404
  145.5 6.7 %collective-permute-start.10 = (bf16[2,128,512]{2,1,0:T(8,128)(2,1)S(1)}, bf16[2,128,512]{2,1,0:T(8,128)(2,1)S(1)}, u32[]{:S(2)}, u32[]{:S(2)}) collective-permute-start(bf16[2,128,512]{2,1,0:T(8,128)(2,1)S(1)} %copy-done.14), channel_id=1, source_target_pairs={{0,3},{1,0},{2,1},{3,2},{4,7},{5,4},{6,5},{7,6},{8,11},{9,8},{10,9... | collective-permute-start | bytes 786440 | tf_op jit(solution)/shard_map/ppermute | solution.py:367
  152.1 0.0 collective-permute-start.11
  152.2 3.2 %collective-permute-start.12 = (bf16[2,128,512]{2,1,0:T(8,128)(2,1)S(1)}, bf16[2,128,512]{2,1,0:T(8,128)(2,1)S(1)}, u32[]{:S(2)}, u32[]{:S(2)}) collective-permute-start(bf16[2,128,512]{2,1,0:T(8,128)(2,1)S(1)} %copy-done.12), channel_id=1, source_target_pairs={{0,2},{1,3},{2,0},{3,1},{4,6},{5,7},{6,4},{7,5},{8,10},{9,11},{10,... | collective-permute-start | bytes 786440 | tf_op jit(solution)/shard_map/ppermute | solution.py:367
  155.4 7.6 %collective-permute-done.10.refs_1_ = bf16[2,128,512]{2,1,0:T(8,128)(2,1)S(1)} collective-permute-done((bf16[2,128,512]{2,1,0:T(8,128)(2,1)S(1)}, bf16[2,128,512]{2,1,0:T(8,128)(2,1)S(1)}, u32[]{:S(2)}, u32[]{:S(2)}) %collective-permute-start.10) | collective-permute-done | bytes 262176 | tf_op jit(solution)/shard_map/ppermute | solution.py:367
  163.0 0.0 collective-permute-done.11.refs_2_
  163.0 3.6 %collective-permute-done.12.refs_3_ = bf16[2,128,512]{2,1,0:T(8,128)(2,1)S(1)} collective-permute-done((bf16[2,128,512]{2,1,0:T(8,128)(2,1)S(1)}, bf16[2,128,512]{2,1,0:T(8,128)(2,1)S(1)}, u32[]{:S(2)}, u32[]{:S(2)}) %collective-permute-start.12) | collective-permute-done | bytes 262176 | tf_op jit(solution)/shard_map/ppermute | solution.py:367
  166.7 0.0 copy-done.1
  166.7 0.7 copy-done.3
  167.4 2.2 %finish_queries.1 = bf16[128,1024]{1,0:T(8,128)(2,1)} custom-call(f32[2,128,512]{2,1,0:T(8,128)} %get-tuple-element.35.refs_0_, bf16[2,128,512]{2,1,0:T(8,128)(2,1)} %copy-done.1, bf16[2,128,512]{2,1,0:T(8,128)(2,1)} %copy-done.2, bf16[2,128,512]{2,1,0:T(8,128)(2,1)} %copy-done.3), custom_call_target="tpu_custom_call" | custom-call | tf_op jit(solution)/shard_map/finish_queries/pallas_call | solution.py:94
  169.5 0.0 all-to-all-done.1
  169.5 0.1 convert_reduce_fusion
  169.7 0.7 fusion.7
  (32 shorter events, 0.1 us)
Async XLA Ops:
  1.4 17.4 %copy-start.4 = (s32[256]{0:T(256)S(1)}, s32[256]{0:T(256)}, u32[]{:S(2)}) copy-start(s32[256]{0:T(256)} %param.11) | copy-start | bytes 3076
  2.5 25.0 %all-to-all-start = ((bf16[16,128,256]{2,1,0:T(8,128)(2,1)}), bf16[16,128,256]{2,1,0:T(8,128)(2,1)S(1)}, u32[]{:S(2)}, u32[]{:S(2)}) async-start(bf16[16,128,256]{2,1,0:T(8,128)(2,1)} %tile.2), calls=%async_computation | async-start | bytes 2097152 | tf_op jit(solution)/shard_map/all_to_all | solution.py:380
  13.1 19.4 %collective-permute-start.2 = (bf16[2,512,128]{2,1,0:T(8,128)(2,1)}, bf16[2,512,128]{2,1,0:T(8,128)(2,1)S(1)}, u32[]{:S(2)}, u32[]{:S(2)}) collective-permute-start(bf16[2,512,128]{2,1,0:T(8,128)(2,1)} %get-tuple-element.22.refs_0_), channel_id=1, source_target_pairs={{0,3},{1,0},{2,1},{3,2},{4,7},{5,4},{6,5},{7,6},{8,11},{9,8},{10,9... | collective-permute-start | bytes 786440 | tf_op jit(solution)/shard_map/ppermute | solution.py:367
  15.8 19.6 %collective-permute-start.1 = (bf16[2,512,128]{2,1,0:T(8,128)(2,1)}, bf16[2,512,128]{2,1,0:T(8,128)(2,1)S(1)}, u32[]{:S(2)}, u32[]{:S(2)}) collective-permute-start(bf16[2,512,128]{2,1,0:T(8,128)(2,1)} %get-tuple-element.22.refs_0_), channel_id=1, source_target_pairs={{0,2},{1,3},{2,0},{3,1},{4,6},{5,7},{6,4},{7,5},{8,10},{9,11},{10,... | collective-permute-start | bytes 786440 | tf_op jit(solution)/shard_map/ppermute | solution.py:367
  16.1 19.7 %collective-permute-start = (bf16[2,512,128]{2,1,0:T(8,128)(2,1)}, bf16[2,512,128]{2,1,0:T(8,128)(2,1)S(1)}, u32[]{:S(2)}, u32[]{:S(2)}) collective-permute-start(bf16[2,512,128]{2,1,0:T(8,128)(2,1)} %get-tuple-element.22.refs_0_), channel_id=1, source_target_pairs={{0,1},{1,2},{2,3},{3,0},{4,5},{5,6},{6,7},{7,4},{8,9},{9,10},{10,1... | collective-permute-start | bytes 786440 | tf_op jit(solution)/shard_map/ppermute | solution.py:367
  16.8 53.9 %collective-permute-start.6 = (bf16[2,528,128]{2,1,0:T(8,128)(2,1)}, bf16[2,528,128]{2,1,0:T(8,128)(2,1)S(1)}, u32[]{:S(2)}, u32[]{:S(2)}) collective-permute-start(bf16[2,528,128]{2,1,0:T(8,128)(2,1)} %get-tuple-element.23.refs_4_), channel_id=1, source_target_pairs={{0,3},{1,0},{2,1},{3,2},{4,7},{5,4},{6,5},{7,6},{8,11},{9,8},{10,9... | collective-permute-start | bytes 811016 | tf_op jit(solution)/shard_map/ppermute | solution.py:367
  27.5 8.3 %copy-start = (bf16[16,128,256]{2,1,0:T(8,128)(2,1)}, bf16[16,128,256]{2,1,0:T(8,128)(2,1)S(1)}, u32[]{:S(2)}) copy-start(bf16[16,128,256]{2,1,0:T(8,128)(2,1)S(1)} %all-to-all-done) | copy-start | bytes 3145732
  27.5 8.3 %collective-permute-start.3 = (bf16[2048,256]{1,0:T(8,128)(2,1)S(1)}, bf16[2048,256]{1,0:T(8,128)(2,1)S(1)}, u32[]{:S(2)}, u32[]{:S(2)}) collective-permute-start(bf16[2048,256]{1,0:T(8,128)(2,1)S(1)} %bitcast.15), channel_id=1, source_target_pairs={{0,8},{8,0},{1,9},{9,1},{2,10},{10,2},{3,11},{11,3},{4,12},{12,4},... | collective-permute-start | bytes 3145736 | tf_op jit(solution)/shard_map/ppermute | solution.py:367
  32.5 3.3 %copy-start.9 = (bf16[2,512,128]{2,1,0:T(8,128)(2,1)}, bf16[2,512,128]{2,1,0:T(8,128)(2,1)S(1)}, u32[]{:S(2)}) copy-start(bf16[2,512,128]{2,1,0:T(8,128)(2,1)S(1)} %collective-permute-done.2.refs_3_) | copy-start | bytes 786436
  32.5 38.3 %collective-permute-start.5 = (bf16[2,528,128]{2,1,0:T(8,128)(2,1)}, bf16[2,528,128]{2,1,0:T(8,128)(2,1)S(1)}, u32[]{:S(2)}, u32[]{:S(2)}) collective-permute-start(bf16[2,528,128]{2,1,0:T(8,128)(2,1)} %get-tuple-element.23.refs_4_), channel_id=1, source_target_pairs={{0,2},{1,3},{2,0},{3,1},{4,6},{5,7},{6,4},{7,5},{8,10},{9,11},{10,... | collective-permute-start | bytes 811016 | tf_op jit(solution)/shard_map/ppermute | solution.py:367
  35.4 0.7 copy-start.10
  35.4 35.4 %collective-permute-start.4 = (bf16[2,528,128]{2,1,0:T(8,128)(2,1)}, bf16[2,528,128]{2,1,0:T(8,128)(2,1)S(1)}, u32[]{:S(2)}, u32[]{:S(2)}) collective-permute-start(bf16[2,528,128]{2,1,0:T(8,128)(2,1)} %get-tuple-element.23.refs_4_), channel_id=1, source_target_pairs={{0,1},{1,2},{2,3},{3,0},{4,5},{5,6},{6,7},{7,4},{8,9},{9,10},{10,1... | collective-permute-start | bytes 811016 | tf_op jit(solution)/shard_map/ppermute | solution.py:367
  35.8 0.8 copy-start.11
  36.6 1.0 copy-start.5
  70.8 14.5 %copy-start.6 = (bf16[2,528,128]{2,1,0:T(8,128)(2,1)}, bf16[2,528,128]{2,1,0:T(8,128)(2,1)S(1)}, u32[]{:S(2)}) copy-start(bf16[2,528,128]{2,1,0:T(8,128)(2,1)S(1)} %collective-permute-done.6.refs_7_) | copy-start | bytes 811012
  70.8 14.5 %copy-start.7 = (bf16[2,528,128]{2,1,0:T(8,128)(2,1)}, bf16[2,528,128]{2,1,0:T(8,128)(2,1)S(1)}, u32[]{:S(2)}) copy-start(bf16[2,528,128]{2,1,0:T(8,128)(2,1)S(1)} %collective-permute-done.5.refs_6_) | copy-start | bytes 811012
  70.8 14.5 %copy-start.8 = (bf16[2,528,128]{2,1,0:T(8,128)(2,1)}, bf16[2,528,128]{2,1,0:T(8,128)(2,1)S(1)}, u32[]{:S(2)}) copy-start(bf16[2,528,128]{2,1,0:T(8,128)(2,1)S(1)} %collective-permute-done.4.refs_5_) | copy-start | bytes 811012
  70.8 13.4 %collective-permute-start.9 = (f32[8,512]{1,0:T(8,128)}, f32[8,512]{1,0:T(8,128)S(1)}, u32[]{:S(2)}, u32[]{:S(2)}) collective-permute-start(f32[8,512]{1,0:T(8,128)} %get-tuple-element.31.refs_8_), channel_id=1, source_target_pairs={{0,1},{1,2},{2,3},{3,0},{4,5},{5,6},{6,7},{7,4},{8,9},{9,10},{10,1... | collective-permute-start | bytes 49160 | tf_op jit(solution)/shard_map/ppermute | solution.py:367
  74.5 9.7 %collective-permute-start.8 = (f32[8,512]{1,0:T(8,128)}, f32[8,512]{1,0:T(8,128)S(1)}, u32[]{:S(2)}, u32[]{:S(2)}) collective-permute-start(f32[8,512]{1,0:T(8,128)} %get-tuple-element.31.refs_8_), channel_id=1, source_target_pairs={{0,2},{1,3},{2,0},{3,1},{4,6},{5,7},{6,4},{7,5},{8,10},{9,11},{10,... | collective-permute-start | bytes 49160 | tf_op jit(solution)/shard_map/ppermute | solution.py:367
  82.2 3.1 %collective-permute-start.7 = (f32[8,512]{1,0:T(8,128)}, f32[8,512]{1,0:T(8,128)S(1)}, u32[]{:S(2)}, u32[]{:S(2)}) collective-permute-start(f32[8,512]{1,0:T(8,128)} %get-tuple-element.31.refs_8_), channel_id=1, source_target_pairs={{0,3},{1,0},{2,1},{3,2},{4,7},{5,4},{6,5},{7,6},{8,11},{9,8},{10,9... | collective-permute-start | bytes 49160 | tf_op jit(solution)/shard_map/ppermute | solution.py:367
  84.2 1.1 copy-start.15
  84.2 1.1 copy-start.16
  85.3 0.6 copy-start.17
  115.1 2.9 %collective-permute-start.13 = (bf16[2048,256]{1,0:T(8,128)(2,1)}, bf16[2048,256]{1,0:T(8,128)(2,1)S(1)}, u32[]{:S(2)}, u32[]{:S(2)}) collective-permute-start(bf16[2048,256]{1,0:T(8,128)(2,1)} %get-tuple-element.40), channel_id=1, source_target_pairs={{0,8},{8,0},{1,9},{9,1},{2,10},{10,2},{3,11},{11,3},{4,12},{12,4},... | collective-permute-start | bytes 3145736 | tf_op jit(solution)/shard_map/ppermute | solution.py:367
  120.9 24.6 %copy-start.14 = (bf16[2,128,512]{2,1,0:T(8,128)(2,1)S(1)}, bf16[2,128,512]{2,1,0:T(8,128)(2,1)}, u32[]{:S(2)}) copy-start(bf16[2,128,512]{2,1,0:T(8,128)(2,1)} %get-tuple-element.36) | copy-start | bytes 786436
  120.9 31.3 %copy-start.13 = (bf16[2,128,512]{2,1,0:T(8,128)(2,1)S(1)}, bf16[2,128,512]{2,1,0:T(8,128)(2,1)}, u32[]{:S(2)}) copy-start(bf16[2,128,512]{2,1,0:T(8,128)(2,1)} %get-tuple-element.37) | copy-start | bytes 786436
  120.9 31.3 %copy-start.12 = (bf16[2,128,512]{2,1,0:T(8,128)(2,1)S(1)}, bf16[2,128,512]{2,1,0:T(8,128)(2,1)}, u32[]{:S(2)}) copy-start(bf16[2,128,512]{2,1,0:T(8,128)(2,1)} %get-tuple-element.38) | copy-start | bytes 786436
  120.9 48.7 %all-to-all-start.1 = ((bf16[16,128,256]{2,1,0:T(8,128)(2,1)}), bf16[16,128,256]{2,1,0:T(8,128)(2,1)S(1)}, u32[]{:S(2)}, u32[]{:S(2)}) async-start(bf16[16,128,256]{2,1,0:T(8,128)(2,1)} %bitcast.7), calls=%async_computation.1 | async-start | bytes 2097152 | tf_op jit(solution)/shard_map/all_to_all | solution.py:404
  145.5 17.5 %collective-permute-start.10 = (bf16[2,128,512]{2,1,0:T(8,128)(2,1)S(1)}, bf16[2,128,512]{2,1,0:T(8,128)(2,1)S(1)}, u32[]{:S(2)}, u32[]{:S(2)}) collective-permute-start(bf16[2,128,512]{2,1,0:T(8,128)(2,1)S(1)} %copy-done.14), channel_id=1, source_target_pairs={{0,3},{1,0},{2,1},{3,2},{4,7},{5,4},{6,5},{7,6},{8,11},{9,8},{10,9... | collective-permute-start | bytes 786440 | tf_op jit(solution)/shard_map/ppermute | solution.py:367
  152.1 10.9 %collective-permute-start.11 = (bf16[2,128,512]{2,1,0:T(8,128)(2,1)S(1)}, bf16[2,128,512]{2,1,0:T(8,128)(2,1)S(1)}, u32[]{:S(2)}, u32[]{:S(2)}) collective-permute-start(bf16[2,128,512]{2,1,0:T(8,128)(2,1)S(1)} %copy-done.13), channel_id=1, source_target_pairs={{0,1},{1,2},{2,3},{3,0},{4,5},{5,6},{6,7},{7,4},{8,9},{9,10},{10,1... | collective-permute-start | bytes 786440 | tf_op jit(solution)/shard_map/ppermute | solution.py:367
  152.2 14.5 %collective-permute-start.12 = (bf16[2,128,512]{2,1,0:T(8,128)(2,1)S(1)}, bf16[2,128,512]{2,1,0:T(8,128)(2,1)S(1)}, u32[]{:S(2)}, u32[]{:S(2)}) collective-permute-start(bf16[2,128,512]{2,1,0:T(8,128)(2,1)S(1)} %copy-done.12), channel_id=1, source_target_pairs={{0,2},{1,3},{2,0},{3,1},{4,6},{5,7},{6,4},{7,5},{8,10},{9,11},{10,... | collective-permute-start | bytes 786440 | tf_op jit(solution)/shard_map/ppermute | solution.py:367
  163.0 3.7 %copy-start.1 = (bf16[2,128,512]{2,1,0:T(8,128)(2,1)}, bf16[2,128,512]{2,1,0:T(8,128)(2,1)S(1)}, u32[]{:S(2)}) copy-start(bf16[2,128,512]{2,1,0:T(8,128)(2,1)S(1)} %collective-permute-done.10.refs_1_) | copy-start | bytes 786436
  163.0 3.7 %copy-start.2 = (bf16[2,128,512]{2,1,0:T(8,128)(2,1)}, bf16[2,128,512]{2,1,0:T(8,128)(2,1)S(1)}, u32[]{:S(2)}) copy-start(bf16[2,128,512]{2,1,0:T(8,128)(2,1)S(1)} %collective-permute-done.11.refs_2_) | copy-start | bytes 786436
  166.7 0.7 copy-start.3

commit v4 on v3

--- a/solution.py
+++ b/solution.py
@@ -13,6 +13,7 @@
 BLOCK = 64
 ROWS = HEADS * BLOCK
 GRAD_ROWS = ROWS + 16
+DEPTH = 3
 SCALE = DH ** -0.5
 C2 = SCALE * math.log2(math.e)
 NEG = -1e30
@@ -23,6 +24,7 @@
 F32 = jnp.float32
 BF16 = jnp.bfloat16
 KEY_AXES = ("x", "zl", "zh")
+ANY = pl.BlockSpec(memory_space=pl.ANY)
 SMEM = pl.BlockSpec(memory_space=pltpu.SMEM)
 VMEM = pl.BlockSpec(memory_space=pltpu.VMEM)
 
@@ -138,7 +140,12 @@
 
 
 def list_size(nq, nk):
-    return nq * ((nk + KB - 1) // KB) + UNROLL + 2
+    most = nq * ((nk + KB - 1) // KB) + 1
+    return (most + UNROLL - 1) // UNROLL * UNROLL + 1
+
+
+def group_count(nq, nk):
+    return list_size(nq, nk) // UNROLL
 
 
 def make_table(rank, place, query_place, key_place):
@@ -159,21 +166,38 @@
     return jnp.concatenate([rank, place, visible, query_place, *lists, end])
 
 
-def run_work(end, prepare, use):
-    def steps(unroll, first):
-        def body(i, c):
-            for u in range(unroll):
-                w = first + i * unroll + u
+def run_work(end, prepare, use, before, after):
+    def body(i, c):
+        slot = lax.rem(i, DEPTH)
+        before(i, slot)
+        for u in range(UNROLL):
+            prepare(i * UNROLL + u + 1, (u + 1) % 2)
+            use(i * UNROLL + u, u % 2, (slot, u))
+        after(i, slot)
+        return c
+
+    whole = end // UNROLL
+    lax.fori_loop(0, whole, body, 0)
+    rest = end - whole * UNROLL
+
+    @pl.when(rest > 0)
+    def _():
+        slot = lax.rem(whole, DEPTH)
+        before(whole, slot)
+
+        def pair(i, c):
+            for u in range(2):
+                w = whole * UNROLL + 2 * i + u
                 prepare(w + 1, (u + 1) % 2)
-                use(w, u % 2)
+                use(w, u % 2, (slot, 2 * i + u))
             return c
 
-        return body
-
-    long = end // UNROLL
-    lax.fori_loop(0, long, steps(UNROLL, 0), 0)
-    rest = long * UNROLL
-    lax.fori_loop(0, (end - rest + 1) // 2, steps(2, rest), 0)
+        lax.fori_loop(0, (rest + 1) // 2, pair, 0)
+        after(whole, slot)
+
+
+def bodies(end):
+    return (end + UNROLL - 1) // UNROLL
 
 
 def difference():
@@ -199,7 +223,7 @@
 def lse_kernel(nq, nk, table_ref, *refs):
     table = Table(table_ref, nq, nk)
     pieces, columns, refs = refs[:4], refs[4:6], refs[6:]
-    lse_ref, ks, vs, kst, q_all, s_buf, diff, l8, m8 = refs
+    lse_ref, shift_ref, e_ref, ks, vs, kst, q_all, s_buf, diff, l8, m8, e_buf, e_sem = refs
     for i, column in enumerate(columns):
         sort_blocks(table, column, slice(0, DH), ks, i * nk // 2, nk // 2)
         sort_blocks(table, column, slice(DH, 2 * DH), vs, i * nk // 2, nk // 2)
@@ -209,17 +233,35 @@
     diff[...] = difference()
     l8[...] = jnp.zeros_like(l8)
 
+    def send(i, slot):
+        return pltpu.make_async_copy(e_buf.at[slot], e_ref.at[i], e_sem.at[slot])
+
+    def free(i, slot):
+        @pl.when(i >= DEPTH)
+        def _():
+            send(i, slot).wait()
+
     def prepare(w, slot):
         b, t, _ = table.entry(w)
         keys = ks[pl.ds(pl.multiple_of(t * KT, KT), KT), :]
         s_buf[slot] = nt(keys, q_all[b])
 
-    def use(w, slot):
+    def use(w, slot, ring):
         b, t, qp = table.entry(w)
-        s = causal(s_buf[slot] * C2, table, t, qp, diff[...])
-        l8[b] += jnp.sum(jnp.exp2(s).reshape(KT // 8, 8, ROWS), axis=0)
-
-    run_work(table.end(), prepare, use)
+        e = jnp.exp2(causal(s_buf[slot] * C2, table, t, qp, diff[...]))
+        l8[b] += jnp.sum(e.reshape(KT // 8, 8, ROWS), axis=0)
+        e_buf[ring] = e.astype(BF16)
+
+    run_work(
+        table.end(), prepare, use, free, lambda i, slot: send(i, slot).start()
+    )
+    for slot in range(DEPTH):
+
+        @pl.when(slot < bodies(table.end()))
+        def _():
+            send(slot, slot).wait()
+
+    shift_ref[...] = jnp.zeros_like(shift_ref)
     fine = jnp.ones((1, ROWS), F32)
     for b in range(nq):
         total = jnp.sum(l8[b], axis=0, keepdims=True)
@@ -248,10 +290,25 @@
             m = m8[...]
             top = jnp.max(m, axis=0, keepdims=True)
             total = jnp.sum(l8[0] * jnp.exp2(m - top), axis=0, keepdims=True)
-            lse_ref[pl.ds(b, 1), :] = jnp.where(table.visible(b) > 0, top + jnp.log2(total), NEG)
+            lse = jnp.where(table.visible(b) > 0, top + jnp.log2(total), NEG)
+            lse_ref[pl.ds(b, 1), :] = lse
+            shift_ref[pl.ds(b, 1), :] = lse
             return c
 
         lax.fori_loop(0, nq, block, 0)
+
+        def entry(w, c):
+            b, t, qp = table.entry(w)
+            keys = ks[pl.ds(pl.multiple_of(t * KT, KT), KT), :]
+            s = nt(keys, q_all[b]) * C2 - lse_ref[pl.ds(b, 1), :]
+            e_buf[0, 0] = jnp.exp2(causal(s, table, t, qp, diff[...])).astype(BF16)
+            place = e_ref.at[w // UNROLL, lax.rem(w, UNROLL)]
+            copy = pltpu.make_async_copy(e_buf.at[0, 0], place, e_sem.at[0])
+            copy.start()
+            copy.wait()
+            return c
+
+        lax.fori_loop(1, table.end(), entry, 0)
 
 
 def local_lse(table, pieces, columns):
@@ -263,18 +320,22 @@
         functools.partial(lse_kernel, nq, nk),
         out_shape=(
             jax.ShapeDtypeStruct((nq, ROWS), F32),
+            jax.ShapeDtypeStruct((nq, ROWS), F32),
+            jax.ShapeDtypeStruct((group_count(nq, nk), UNROLL, KT, ROWS), BF16),
             row_shape,
             row_shape,
             jax.ShapeDtypeStruct((DH, count), BF16),
         ),
         in_specs=[SMEM] + [VMEM] * 6,
-        out_specs=(VMEM,) * 4,
+        out_specs=(VMEM, VMEM, ANY) + (VMEM,) * 3,
         scratch_shapes=[
             pltpu.VMEM((nq, ROWS, DH), BF16),
             pltpu.VMEM((2, KT, ROWS), F32),
             pltpu.VMEM((BLOCK, ROWS), jnp.int32),
             pltpu.VMEM((nq, 8, ROWS), F32),
             pltpu.VMEM((8, ROWS), F32),
+            pltpu.VMEM((DEPTH, UNROLL, KT, ROWS), BF16),
+            pltpu.SemaphoreType.DMA((DEPTH,)),
         ],
         compiler_params=params(),
         cost_estimate=cost(1, nq, count),
@@ -285,13 +346,25 @@
 def grad_kernel(nq, nk, table_ref, *refs):
     table = Table(table_ref, nq, nk)
     queries, grads, refs = refs[:4], refs[4:8], refs[8:]
-    sums_in, (ks, vs, kst), refs = refs[:4], refs[4:7], refs[7:]
+    sums_in, (shift_ref, e_ref, ks, vs, kst), refs = refs[:4], refs[4:9], refs[9:]
     query_out, kv_out, kv_send, refs = refs[:4], refs[4], refs[5], refs[6:]
-    q_all, g_all, lse, delta, sums, dqa, s_buf, dp_buf, diff = refs
+    q_all, g_all, factor, delta, sums, dqa, dp_buf, e_buf, e_sem = refs
+
+    def fetch(i, slot):
+        return pltpu.make_async_copy(e_ref.at[i], e_buf.at[slot], e_sem.at[slot])
+
+    def fetch_body(i, slot):
+        @pl.when(i < bodies(table.end()))
+        def _():
+            fetch(i, slot).start()
+
+    for slot in range(DEPTH):
+        fetch_body(slot, slot)
     for i in range(4):
         for j in range(2):
             b = 2 * i + j
-            lse[b] = combine([sums_in[d][b2:b2 + 1, :] for d in range(4) for b2 in [2 * ((i + d) % 4) + j]])
+            lse = combine([sums_in[d][b2:b2 + 1, :] for d in range(4) for b2 in [2 * ((i + d) % 4) + j]])
+            factor[b] = jnp.exp2(shift_ref[b:b + 1, :] - lse)
             q_all[b] = queries[i][j]
             g_all[b] = grads[i][j, :ROWS, :]
             tail = grads[i][j, ROWS:, :].astype(F32)
@@ -301,26 +374,29 @@
                 delta[b, :, c * DH:(c + 1) * DH] = tail[c:c + 1]
     sums[...] = jnp.zeros_like(sums)
     dqa[...] = jnp.zeros_like(dqa)
-    s_buf[0] = jnp.zeros((KT, ROWS), F32)
     dp_buf[0] = jnp.zeros((KT, ROWS), F32)
-    diff[...] = difference()
 
     def prepare(w, slot):
         b, t, _ = table.entry(w)
         at = pl.ds(pl.multiple_of(t * KT, KT), KT)
-        s_buf[slot] = nt(ks[at, :], q_all[b])
         dp_buf[slot] = nt(vs[at, :], g_all[b])
 
-    def use(w, slot):
-        b, t, qp = table.entry(w)
+    def use(w, slot, ring):
+        b, t, _ = table.entry(w)
         at = pl.ds(pl.multiple_of(t * KT, KT), KT)
-        p = jnp.exp2(causal(s_buf[slot] * C2 - lse[b], table, t, qp, diff[...]))
+        p = e_buf[ring].astype(F32) * factor[b]
         ds = (p * (dp_buf[slot] - delta[b])).astype(BF16)
         sums[1, at, :] += nn(p.astype(BF16), g_all[b])
         sums[0, at, :] += nn(ds, q_all[b])
         dqa[b] += nn(kst[:, at], ds)
 
-    run_work(table.end(), prepare, use)
+    run_work(
+        table.end(),
+        prepare,
+        use,
+        lambda i, slot: fetch(i, slot).wait(),
+        lambda i, slot: fetch_body(i + DEPTH, slot),
+    )
     for i in range(4):
         for j in range(2):
             query_out[i][j] = (dqa[2 * i + j] * SCALE).astype(query_out[i].dtype)
@@ -336,15 +412,15 @@
         lax.fori_loop(0, nk // 2, body, 0, unroll=2)
 
 
-def local_grads(table, queries, grads, sums, sorted_keys):
+def local_grads(table, queries, grads, sums, results):
     nq = 8
-    count = sorted_keys[0].shape[0]
+    count = results[2].shape[0]
     nk = count // BLOCK
     return pl.pallas_call(
         functools.partial(grad_kernel, nq, nk),
         out_shape=tuple(jax.ShapeDtypeStruct((2, DH, ROWS), F32 if i == 0 else BF16) for i in range(4))
         + tuple(jax.ShapeDtypeStruct((count // 2, 2 * DH), t) for t in (F32, BF16)),
-        in_specs=[SMEM] + [VMEM] * 15,
+        in_specs=[SMEM] + [VMEM] * 13 + [ANY] + [VMEM] * 3,
         out_specs=(VMEM,) * 6,
         scratch_shapes=[
             pltpu.VMEM((nq, ROWS, DH), BF16),
@@ -354,13 +430,13 @@
             pltpu.VMEM((2, count, DH), F32),
             pltpu.VMEM((nq, DH, ROWS), F32),
             pltpu.VMEM((2, KT, ROWS), F32),
-            pltpu.VMEM((2, KT, ROWS), F32),
-            pltpu.VMEM((BLOCK, ROWS), jnp.int32),
+            pltpu.VMEM((DEPTH, UNROLL, KT, ROWS), BF16),
+            pltpu.SemaphoreType.DMA((DEPTH,)),
         ],
         compiler_params=params(),
         cost_estimate=cost(5, nq, count),
         name="local_grads",
-    )(table, *queries, *grads, *sums, *sorted_keys)
+    )(table, *queries, *grads, *sums, *results)
 
 
 def along(axis, shift, size, array):
@@ -395,10 +471,10 @@
     query_pieces = gather_y(query_message)
     grad_pieces = gather_y(grad_message)
 
-    (part, *sorted_keys), grad_pieces[1:] = fence((local_lse(table, query_pieces, columns), grad_pieces[1:]))
+    (part, *results), grad_pieces[1:] = fence((local_lse(table, query_pieces, columns), grad_pieces[1:]))
     sums = [part] + [along("y", -d, 4, part) for d in (1, 2, 3)]
 
-    *query_parts, kv_part, kv_send = local_grads(table, query_pieces, grad_pieces, sums, sorted_keys)
+    *query_parts, kv_part, kv_send = local_grads(table, query_pieces, grad_pieces, sums, results)
     query_parts = [query_parts[0]] + [along("y", -s, 4, query_parts[s]) for s in (1, 3, 2)]
     kv_part = (kv_part + along("core", 1, 2, kv_send).astype(F32)).astype(BF16)
     terms = lax.all_to_all(kv_part, KEY_AXES, 0, 0, tiled=True)

time: 170 us -> 251 us (1.48); the launches traced: 170 us -> 254 us
  Pallas kernels: 66.7 us -> 171 us
  starting transfers between devices: 67.9 us -> 47.4 us
    pallas_call x1, Pallas kernels: 33.2 us -> 135 us  [local_lse(): pl.pallas_call(functools.partial(lse_kernel, nq, nk), out_shape=(jax.Shap...]
    all_to_all x1, starting transfers between devices: 24.6 us -> 13 us  [shards(): terms = lax.all_to_all(kv_part, KEY_AXES, 0, 0, tiled=True)]
    ppermute x14, starting transfers between devices: 34.9 us -> 26 us  [along(): lax.ppermute(array, axis, [(i, (i + shift) % size) for i in range(size)])]
    pallas_call x1, Pallas kernels: 29.2 us -> 32 us  [local_grads(): pl.pallas_call(functools.partial(grad_kernel, nq, nk), out_shape=tuple((j...]
  transfers between devices with their start and end apart: 16 -> 16, of which waited for: 5 -> 6; matrix products, arithmetic and copies ran while one was open for 1% -> 1% of each run, Pallas kernels for 22% -> 55%
where the time goes in v4:
time: 251 us; the launch traced here: 254 us
  Pallas kernels  171 us (68%)
  starting transfers between devices  47.4 us (19%)
  waiting for transfers between devices  22.9 us (9%)
  local copies, waits for them, and re-layouts  5.96 us (2%)
  other arithmetic  5.09 us (2%)
    pallas_call x1, Pallas kernels, local_lse(): pl.pallas_call(functools.partial(lse_kernel, nq, nk), out_shape=(jax.Shap...  135 us
    pallas_call x1, Pallas kernels, local_grads(): pl.pallas_call(functools.partial(grad_kernel, nq, nk), out_shape=tuple((j...  32 us
    ppermute x14, starting transfers between devices, along(): lax.ppermute(array, axis, [(i, (i + shift) % size) for i in range(size)])  26 us
    ppermute x14, waiting for transfers between devices, along(): lax.ppermute(array, axis, [(i, (i + shift) % size) for i in range(size)])  15 us
    all_to_all x1, starting transfers between devices, shards(): terms = lax.all_to_all(kv_part, KEY_AXES, 0, 0, tiled=True)  13 us
    all_to_all x1, starting transfers between devices, shards(): column = lax.all_to_all(jnp.tile(pair, (16, 1)), KEY_AXES, 0, 0, tiled=True)  8.43 us
    all_to_all x1, waiting for transfers between devices, shards(): column = lax.all_to_all(jnp.tile(pair, (16, 1)), KEY_AXES, 0, 0, tiled=True)  7.97 us
  transfers between devices with their start and end apart: 16, of which 6 were waited for; matrix products, arithmetic and copies ran while one was open for 1% of the time, Pallas kernels for 55%

profile of v4, /device:TPU:1, one launch (start us, length us, event | category | flops | bytes accessed | tf_op | source)
XLA Modules:
  0.0 254.0 jit_solution(10859582353805017560)
XLA Ops:
  0.6 0.8 pad_maximum_fusion
  1.4 1.1 tile.2
  2.5 8.4 %all-to-all-start = ((bf16[16,128,256]{2,1,0:T(8,128)(2,1)}), bf16[16,128,256]{2,1,0:T(8,128)(2,1)S(1)}, u32[]{:S(2)}, u32[]{:S(2)}) async-start(bf16[16,128,256]{2,1,0:T(8,128)(2,1)} %tile.2), calls=%async_computation | async-start | bytes 2097152 | tf_op jit(solution)/shard_map/all_to_all | solution.py:456
  10.9 2.1 make_messages.1
  13.0 2.7 %collective-permute-start.2 = (bf16[2,512,128]{2,1,0:T(8,128)(2,1)}, bf16[2,512,128]{2,1,0:T(8,128)(2,1)S(1)}, u32[]{:S(2)}, u32[]{:S(2)}) collective-permute-start(bf16[2,512,128]{2,1,0:T(8,128)(2,1)} %get-tuple-element.26.refs_0_), channel_id=1, source_target_pairs={{0,3},{1,0},{2,1},{3,2},{4,7},{5,4},{6,5},{7,6},{8,11},{9,8},{10,9... | collective-permute-start | bytes 786440 | tf_op jit(solution)/shard_map/ppermute | solution.py:443
  15.8 0.3 collective-permute-start.1
  16.1 0.7 collective-permute-start
  16.8 2.0 collective-permute-start.6
  18.8 0.0 copy-done.4
  18.8 0.2 reshape.68
  19.0 0.1 reshape.69
  19.2 0.1 le.16
  19.3 0.1 lt.72
  19.4 0.2 convert_reduce_fusion.2
  19.5 8.0 %all-to-all-done = bf16[16,128,256]{2,1,0:T(8,128)(2,1)S(1)} async-done(((bf16[16,128,256]{2,1,0:T(8,128)(2,1)}), bf16[16,128,256]{2,1,0:T(8,128)(2,1)S(1)}, u32[]{:S(2)}, u32[]{:S(2)}) %all-to-all-start) | async-done | bytes 1048608 | tf_op jit(solution)/shard_map/all_to_all | solution.py:456
  27.5 2.6 %collective-permute-start.3 = (bf16[2048,256]{1,0:T(8,128)(2,1)S(1)}, bf16[2048,256]{1,0:T(8,128)(2,1)S(1)}, u32[]{:S(2)}, u32[]{:S(2)}) collective-permute-start(bf16[2048,256]{1,0:T(8,128)(2,1)S(1)} %bitcast.15), channel_id=1, source_target_pairs={{0,8},{8,0},{1,9},{9,1},{2,10},{10,2},{3,11},{11,3},{4,12},{12,4},... | collective-permute-start | bytes 3145736 | tf_op jit(solution)/shard_map/ppermute | solution.py:443
  30.1 0.6 fusion.6
  30.7 0.1 select_reduce_fusion.4
  30.8 0.1 convert_reduce_fusion.1
  30.9 0.1 select_reduce_fusion.1
  31.0 0.1 select_reduce_fusion
  31.8 0.7 concatenate.6.table_ref
  32.5 0.0 collective-permute-done.2.refs_3_
  32.5 2.9 %collective-permute-start.5 = (bf16[2,528,128]{2,1,0:T(8,128)(2,1)}, bf16[2,528,128]{2,1,0:T(8,128)(2,1)S(1)}, u32[]{:S(2)}, u32[]{:S(2)}) collective-permute-start(bf16[2,528,128]{2,1,0:T(8,128)(2,1)} %get-tuple-element.27.refs_4_), channel_id=1, source_target_pairs={{0,2},{1,3},{2,0},{3,1},{4,6},{5,7},{6,4},{7,5},{8,10},{9,11},{10,... | collective-permute-start | bytes 811016 | tf_op jit(solution)/shard_map/ppermute | solution.py:443
  35.4 0.0 collective-permute-done.1.refs_2_
  35.4 0.4 collective-permute-start.4
  35.8 0.0 collective-permute-done.refs_1_
  35.8 0.0 collective-permute-done.3.refs_5_
  35.8 0.3 copy-done.10
  36.1 0.4 copy-done.11
  36.5 1.0 copy-done.5
  37.5 134.8 %local_lse.1 = (f32[8,512]{1,0:T(8,128)}, f32[8,512]{1,0:T(8,128)}, bf16[17,8,256,512]{3,2,1,0:T(8,128)(2,1)}, bf16[4096,128]{1,0:T(8,128)(2,1)}, bf16[4096,128]{1,0:T(8,128)(2,1)}, /*index=5*/bf16[128,4096]{1,0:T(8,128)(2,1)}) custom-call(s32[556]{0:T(1024)} %concatenate.6.table_ref, bf16[2,512,128]{2,1,0:T(8,128)(2,1)} %get-tuple-element.26.refs_0_, ...), custom_call_target="tpu_custom_call" | custom-call | flops 4294967296 | bytes 8388608 | tf_op jit(solution)/shard_map/local_lse/pallas_call | solution.py:319
  172.3 0.0 collective-permute-done.6.refs_7_
  172.3 0.0 collective-permute-done.5.refs_6_
  172.3 0.0 copy-start.7
  172.4 0.0 collective-permute-done.4.refs_5_
  172.4 3.1 %collective-permute-start.9 = (f32[8,512]{1,0:T(8,128)}, f32[8,512]{1,0:T(8,128)S(1)}, u32[]{:S(2)}, u32[]{:S(2)}) collective-permute-start(f32[8,512]{1,0:T(8,128)} %get-tuple-element.37.refs_8_), channel_id=1, source_target_pairs={{0,1},{1,2},{2,3},{3,0},{4,5},{5,6},{6,7},{7,4},{8,9},{9,10},{10,1... | collective-permute-start | bytes 49160 | tf_op jit(solution)/shard_map/ppermute | solution.py:443
  175.5 5.4 %collective-permute-start.8 = (f32[8,512]{1,0:T(8,128)}, f32[8,512]{1,0:T(8,128)S(1)}, u32[]{:S(2)}, u32[]{:S(2)}) collective-permute-start(f32[8,512]{1,0:T(8,128)} %get-tuple-element.37.refs_8_), channel_id=1, source_target_pairs={{0,2},{1,3},{2,0},{3,1},{4,6},{5,7},{6,4},{7,5},{8,10},{9,11},{10,... | collective-permute-start | bytes 49160 | tf_op jit(solution)/shard_map/ppermute | solution.py:443
  180.9 2.0 collective-permute-start.7
  182.8 0.0 collective-permute-done.9.refs_11_
  182.8 0.0 collective-permute-done.8.refs_10_
  182.9 0.0 copy-start.16
  182.9 1.1 collective-permute-done.7.refs_9_
  183.9 0.0 copy-done.6
  183.9 0.0 copy-done.16
  183.9 0.0 copy-start.17
  184.0 0.6 copy-done.17
  184.5 32.0 %local_grads.1 = (f32[2,128,512]{2,1,0:T(8,128)}, bf16[2,128,512]{2,1,0:T(8,128)(2,1)}, bf16[2,128,512]{2,1,0:T(8,128)(2,1)}, bf16[2,128,512]{2,1,0:T(8,128)(2,1...) custom-call(s32[556]{0:T(1024)} %concatenate.6.table_ref, bf16[2,512,128]{2,1,0:T(8,128)(2,1)} %get-tuple-element.26.refs_0_, ...), custom_call_target="tpu_custom_call" | custom-call | flops 21474836480 | bytes 8388608 | tf_op jit(solution)/shard_map/local_grads/pallas_call | solution.py:419
  216.5 0.1 collective-permute-start.13
  216.6 2.9 %collective-permute-done.13 = bf16[2048,256]{1,0:T(8,128)(2,1)S(1)} collective-permute-done((bf16[2048,256]{1,0:T(8,128)(2,1)}, bf16[2048,256]{1,0:T(8,128)(2,1)S(1)}, u32[]{:S(2)}, u32[]{:S(2)}) %collective-permute-start.13) | collective-permute-done | bytes 1048608 | tf_op jit(solution)/shard_map/ppermute | solution.py:443
  219.5 2.9 %add_convert_fusion = bf16[2048,256]{1,0:T(8,128)(2,1)} fusion(f32[2048,256]{1,0:T(8,128)} %get-tuple-element.47, bf16[2048,256]{1,0:T(8,128)(2,1)S(1)} %collective-permute-done.13), kind=kLoop, calls=%fused_computation.1 | loop fusion | flops 1572864 | bytes 4194304 | tf_op jit(solution)/shard_map/convert_element_type | solution.py:479
  222.4 13.0 %all-to-all-start.1 = ((bf16[16,128,256]{2,1,0:T(8,128)(2,1)}), bf16[16,128,256]{2,1,0:T(8,128)(2,1)S(1)}, u32[]{:S(2)}, u32[]{:S(2)}) async-start(bf16[16,128,256]{2,1,0:T(8,128)(2,1)} %bitcast.7), calls=%async_computation.1 | async-start | bytes 2097152 | tf_op jit(solution)/shard_map/all_to_all | solution.py:480
  235.4 0.5 collective-permute-start.10
  235.9 0.0 copy-done.13
  235.9 1.0 collective-permute-start.11
  237.0 2.3 collective-permute-start.12
  239.3 3.4 %collective-permute-done.10.refs_1_ = bf16[2,128,512]{2,1,0:T(8,128)(2,1)S(1)} collective-permute-done((bf16[2,128,512]{2,1,0:T(8,128)(2,1)S(1)}, bf16[2,128,512]{2,1,0:T(8,128)(2,1)S(1)}, u32[]{:S(2)}, u32[]{:S(2)}) %collective-permute-start.10) | collective-permute-done | bytes 262176 | tf_op jit(solution)/shard_map/ppermute | solution.py:443
  242.7 1.3 collective-permute-done.11.refs_2_
  244.0 6.3 %collective-permute-done.12.refs_3_ = bf16[2,128,512]{2,1,0:T(8,128)(2,1)S(1)} collective-permute-done((bf16[2,128,512]{2,1,0:T(8,128)(2,1)S(1)}, bf16[2,128,512]{2,1,0:T(8,128)(2,1)S(1)}, u32[]{:S(2)}, u32[]{:S(2)}) %collective-permute-start.12) | collective-permute-done | bytes 262176 | tf_op jit(solution)/shard_map/ppermute | solution.py:443
  250.3 0.7 copy-done.3
  251.0 2.2 finish_queries.1
  253.1 0.0 all-to-all-done.1
  253.1 0.1 convert_reduce_fusion
  253.3 0.7 fusion.7
  (32 shorter events, 0.1 us)
Async XLA Ops:
  1.4 17.4 %copy-start.4 = (s32[256]{0:T(256)S(1)}, s32[256]{0:T(256)}, u32[]{:S(2)}) copy-start(s32[256]{0:T(256)} %param.11) | copy-start | bytes 3076
  2.5 25.0 %all-to-all-start = ((bf16[16,128,256]{2,1,0:T(8,128)(2,1)}), bf16[16,128,256]{2,1,0:T(8,128)(2,1)S(1)}, u32[]{:S(2)}, u32[]{:S(2)}) async-start(bf16[16,128,256]{2,1,0:T(8,128)(2,1)} %tile.2), calls=%async_computation | async-start | bytes 2097152 | tf_op jit(solution)/shard_map/all_to_all | solution.py:456
  13.0 19.4 %collective-permute-start.2 = (bf16[2,512,128]{2,1,0:T(8,128)(2,1)}, bf16[2,512,128]{2,1,0:T(8,128)(2,1)S(1)}, u32[]{:S(2)}, u32[]{:S(2)}) collective-permute-start(bf16[2,512,128]{2,1,0:T(8,128)(2,1)} %get-tuple-element.26.refs_0_), channel_id=1, source_target_pairs={{0,3},{1,0},{2,1},{3,2},{4,7},{5,4},{6,5},{7,6},{8,11},{9,8},{10,9... | collective-permute-start | bytes 786440 | tf_op jit(solution)/shard_map/ppermute | solution.py:443
  15.8 19.6 %collective-permute-start.1 = (bf16[2,512,128]{2,1,0:T(8,128)(2,1)}, bf16[2,512,128]{2,1,0:T(8,128)(2,1)S(1)}, u32[]{:S(2)}, u32[]{:S(2)}) collective-permute-start(bf16[2,512,128]{2,1,0:T(8,128)(2,1)} %get-tuple-element.26.refs_0_), channel_id=1, source_target_pairs={{0,2},{1,3},{2,0},{3,1},{4,6},{5,7},{6,4},{7,5},{8,10},{9,11},{10,... | collective-permute-start | bytes 786440 | tf_op jit(solution)/shard_map/ppermute | solution.py:443
  16.1 19.7 %collective-permute-start = (bf16[2,512,128]{2,1,0:T(8,128)(2,1)}, bf16[2,512,128]{2,1,0:T(8,128)(2,1)S(1)}, u32[]{:S(2)}, u32[]{:S(2)}) collective-permute-start(bf16[2,512,128]{2,1,0:T(8,128)(2,1)} %get-tuple-element.26.refs_0_), channel_id=1, source_target_pairs={{0,1},{1,2},{2,3},{3,0},{4,5},{5,6},{6,7},{7,4},{8,9},{9,10},{10,1... | collective-permute-start | bytes 786440 | tf_op jit(solution)/shard_map/ppermute | solution.py:443
  16.8 155.5 %collective-permute-start.6 = (bf16[2,528,128]{2,1,0:T(8,128)(2,1)}, bf16[2,528,128]{2,1,0:T(8,128)(2,1)S(1)}, u32[]{:S(2)}, u32[]{:S(2)}) collective-permute-start(bf16[2,528,128]{2,1,0:T(8,128)(2,1)} %get-tuple-element.27.refs_4_), channel_id=1, source_target_pairs={{0,3},{1,0},{2,1},{3,2},{4,7},{5,4},{6,5},{7,6},{8,11},{9,8},{10,9... | collective-permute-start | bytes 811016 | tf_op jit(solution)/shard_map/ppermute | solution.py:443
  27.5 8.3 %copy-start = (bf16[16,128,256]{2,1,0:T(8,128)(2,1)}, bf16[16,128,256]{2,1,0:T(8,128)(2,1)S(1)}, u32[]{:S(2)}) copy-start(bf16[16,128,256]{2,1,0:T(8,128)(2,1)S(1)} %all-to-all-done) | copy-start | bytes 3145732
  27.5 8.3 %collective-permute-start.3 = (bf16[2048,256]{1,0:T(8,128)(2,1)S(1)}, bf16[2048,256]{1,0:T(8,128)(2,1)S(1)}, u32[]{:S(2)}, u32[]{:S(2)}) collective-permute-start(bf16[2048,256]{1,0:T(8,128)(2,1)S(1)} %bitcast.15), channel_id=1, source_target_pairs={{0,8},{8,0},{1,9},{9,1},{2,10},{10,2},{3,11},{11,3},{4,12},{12,4},... | collective-permute-start | bytes 3145736 | tf_op jit(solution)/shard_map/ppermute | solution.py:443
  32.5 3.3 %copy-start.9 = (bf16[2,512,128]{2,1,0:T(8,128)(2,1)}, bf16[2,512,128]{2,1,0:T(8,128)(2,1)S(1)}, u32[]{:S(2)}) copy-start(bf16[2,512,128]{2,1,0:T(8,128)(2,1)S(1)} %collective-permute-done.2.refs_3_) | copy-start | bytes 786436
  32.5 139.9 %collective-permute-start.5 = (bf16[2,528,128]{2,1,0:T(8,128)(2,1)}, bf16[2,528,128]{2,1,0:T(8,128)(2,1)S(1)}, u32[]{:S(2)}, u32[]{:S(2)}) collective-permute-start(bf16[2,528,128]{2,1,0:T(8,128)(2,1)} %get-tuple-element.27.refs_4_), channel_id=1, source_target_pairs={{0,2},{1,3},{2,0},{3,1},{4,6},{5,7},{6,4},{7,5},{8,10},{9,11},{10,... | collective-permute-start | bytes 811016 | tf_op jit(solution)/shard_map/ppermute | solution.py:443
  35.4 0.7 copy-start.10
  35.4 137.0 %collective-permute-start.4 = (bf16[2,528,128]{2,1,0:T(8,128)(2,1)}, bf16[2,528,128]{2,1,0:T(8,128)(2,1)S(1)}, u32[]{:S(2)}, u32[]{:S(2)}) collective-permute-start(bf16[2,528,128]{2,1,0:T(8,128)(2,1)} %get-tuple-element.27.refs_4_), channel_id=1, source_target_pairs={{0,1},{1,2},{2,3},{3,0},{4,5},{5,6},{6,7},{7,4},{8,9},{9,10},{10,1... | collective-permute-start | bytes 811016 | tf_op jit(solution)/shard_map/ppermute | solution.py:443
  35.8 0.7 copy-start.11
  36.5 1.0 copy-start.5
  172.3 11.6 %copy-start.6 = (bf16[2,528,128]{2,1,0:T(8,128)(2,1)}, bf16[2,528,128]{2,1,0:T(8,128)(2,1)S(1)}, u32[]{:S(2)}) copy-start(bf16[2,528,128]{2,1,0:T(8,128)(2,1)S(1)} %collective-permute-done.6.refs_7_) | copy-start | bytes 811012
  172.3 11.6 %copy-start.7 = (bf16[2,528,128]{2,1,0:T(8,128)(2,1)}, bf16[2,528,128]{2,1,0:T(8,128)(2,1)S(1)}, u32[]{:S(2)}) copy-start(bf16[2,528,128]{2,1,0:T(8,128)(2,1)S(1)} %collective-permute-done.5.refs_6_) | copy-start | bytes 811012
  172.4 11.6 %copy-start.8 = (bf16[2,528,128]{2,1,0:T(8,128)(2,1)}, bf16[2,528,128]{2,1,0:T(8,128)(2,1)S(1)}, u32[]{:S(2)}) copy-start(bf16[2,528,128]{2,1,0:T(8,128)(2,1)S(1)} %collective-permute-done.4.refs_5_) | copy-start | bytes 811012
  172.4 10.5 %collective-permute-start.9 = (f32[8,512]{1,0:T(8,128)}, f32[8,512]{1,0:T(8,128)S(1)}, u32[]{:S(2)}, u32[]{:S(2)}) collective-permute-start(f32[8,512]{1,0:T(8,128)} %get-tuple-element.37.refs_8_), channel_id=1, source_target_pairs={{0,1},{1,2},{2,3},{3,0},{4,5},{5,6},{6,7},{7,4},{8,9},{9,10},{10,1... | collective-permute-start | bytes 49160 | tf_op jit(solution)/shard_map/ppermute | solution.py:443
  175.5 7.4 %collective-permute-start.8 = (f32[8,512]{1,0:T(8,128)}, f32[8,512]{1,0:T(8,128)S(1)}, u32[]{:S(2)}, u32[]{:S(2)}) collective-permute-start(f32[8,512]{1,0:T(8,128)} %get-tuple-element.37.refs_8_), channel_id=1, source_target_pairs={{0,2},{1,3},{2,0},{3,1},{4,6},{5,7},{6,4},{7,5},{8,10},{9,11},{10,... | collective-permute-start | bytes 49160 | tf_op jit(solution)/shard_map/ppermute | solution.py:443
  180.9 3.1 %collective-permute-start.7 = (f32[8,512]{1,0:T(8,128)}, f32[8,512]{1,0:T(8,128)S(1)}, u32[]{:S(2)}, u32[]{:S(2)}) collective-permute-start(f32[8,512]{1,0:T(8,128)} %get-tuple-element.37.refs_8_), channel_id=1, source_target_pairs={{0,3},{1,0},{2,1},{3,2},{4,7},{5,4},{6,5},{7,6},{8,11},{9,8},{10,9... | collective-permute-start | bytes 49160 | tf_op jit(solution)/shard_map/ppermute | solution.py:443
  182.8 1.1 copy-start.15
  182.9 1.1 copy-start.16
  183.9 0.6 copy-start.17
  216.5 3.0 %collective-permute-start.13 = (bf16[2048,256]{1,0:T(8,128)(2,1)}, bf16[2048,256]{1,0:T(8,128)(2,1)S(1)}, u32[]{:S(2)}, u32[]{:S(2)}) collective-permute-start(bf16[2048,256]{1,0:T(8,128)(2,1)} %get-tuple-element.48), channel_id=1, source_target_pairs={{0,8},{8,0},{1,9},{9,1},{2,10},{10,2},{3,11},{11,3},{4,12},{12,4},... | collective-permute-start | bytes 3145736 | tf_op jit(solution)/shard_map/ppermute | solution.py:443
  222.4 13.0 %copy-start.14 = (bf16[2,128,512]{2,1,0:T(8,128)(2,1)S(1)}, bf16[2,128,512]{2,1,0:T(8,128)(2,1)}, u32[]{:S(2)}) copy-start(bf16[2,128,512]{2,1,0:T(8,128)(2,1)} %get-tuple-element.44) | copy-start | bytes 786436
  222.4 13.5 %copy-start.13 = (bf16[2,128,512]{2,1,0:T(8,128)(2,1)S(1)}, bf16[2,128,512]{2,1,0:T(8,128)(2,1)}, u32[]{:S(2)}) copy-start(bf16[2,128,512]{2,1,0:T(8,128)(2,1)} %get-tuple-element.45) | copy-start | bytes 786436
  222.4 14.6 %copy-start.12 = (bf16[2,128,512]{2,1,0:T(8,128)(2,1)S(1)}, bf16[2,128,512]{2,1,0:T(8,128)(2,1)}, u32[]{:S(2)}) copy-start(bf16[2,128,512]{2,1,0:T(8,128)(2,1)} %get-tuple-element.46) | copy-start | bytes 786436
  222.4 30.7 %all-to-all-start.1 = ((bf16[16,128,256]{2,1,0:T(8,128)(2,1)}), bf16[16,128,256]{2,1,0:T(8,128)(2,1)S(1)}, u32[]{:S(2)}, u32[]{:S(2)}) async-start(bf16[16,128,256]{2,1,0:T(8,128)(2,1)} %bitcast.7), calls=%async_computation.1 | async-start | bytes 2097152 | tf_op jit(solution)/shard_map/all_to_all | solution.py:480
  235.4 7.3 %collective-permute-start.10 = (bf16[2,128,512]{2,1,0:T(8,128)(2,1)S(1)}, bf16[2,128,512]{2,1,0:T(8,128)(2,1)S(1)}, u32[]{:S(2)}, u32[]{:S(2)}) collective-permute-start(bf16[2,128,512]{2,1,0:T(8,128)(2,1)S(1)} %copy-done.14), channel_id=1, source_target_pairs={{0,3},{1,0},{2,1},{3,2},{4,7},{5,4},{6,5},{7,6},{8,11},{9,8},{10,9... | collective-permute-start | bytes 786440 | tf_op jit(solution)/shard_map/ppermute | solution.py:443
  235.9 8.1 %collective-permute-start.11 = (bf16[2,128,512]{2,1,0:T(8,128)(2,1)S(1)}, bf16[2,128,512]{2,1,0:T(8,128)(2,1)S(1)}, u32[]{:S(2)}, u32[]{:S(2)}) collective-permute-start(bf16[2,128,512]{2,1,0:T(8,128)(2,1)S(1)} %copy-done.13), channel_id=1, source_target_pairs={{0,1},{1,2},{2,3},{3,0},{4,5},{5,6},{6,7},{7,4},{8,9},{9,10},{10,1... | collective-permute-start | bytes 786440 | tf_op jit(solution)/shard_map/ppermute | solution.py:443
  237.0 13.3 %collective-permute-start.12 = (bf16[2,128,512]{2,1,0:T(8,128)(2,1)S(1)}, bf16[2,128,512]{2,1,0:T(8,128)(2,1)S(1)}, u32[]{:S(2)}, u32[]{:S(2)}) collective-permute-start(bf16[2,128,512]{2,1,0:T(8,128)(2,1)S(1)} %copy-done.12), channel_id=1, source_target_pairs={{0,2},{1,3},{2,0},{3,1},{4,6},{5,7},{6,4},{7,5},{8,10},{9,11},{10,... | collective-permute-start | bytes 786440 | tf_op jit(solution)/shard_map/ppermute | solution.py:443
  242.7 7.6 %copy-start.1 = (bf16[2,128,512]{2,1,0:T(8,128)(2,1)}, bf16[2,128,512]{2,1,0:T(8,128)(2,1)S(1)}, u32[]{:S(2)}) copy-start(bf16[2,128,512]{2,1,0:T(8,128)(2,1)S(1)} %collective-permute-done.10.refs_1_) | copy-start | bytes 786436
  244.0 6.3 %copy-start.2 = (bf16[2,128,512]{2,1,0:T(8,128)(2,1)}, bf16[2,128,512]{2,1,0:T(8,128)(2,1)S(1)}, u32[]{:S(2)}) copy-start(bf16[2,128,512]{2,1,0:T(8,128)(2,1)S(1)} %collective-permute-done.11.refs_2_) | copy-start | bytes 786436
  250.3 0.7 copy-start.3
